TPU v7x, 256 devices: a whole 4x4x8 slice. The times are simulated.
256 devices in a mesh: gx: 16 (over z, x_hi), gy: 16 (over x_lo, y, core).
Axes of the slice: x: 4 (x_hi: 2, x_lo: 2; x = x_hi * 2 + x_lo), y: 4, z: 8, core: 2. Of those that a mesh axis runs over, the one named last changes fastest.
Arguments:
- coarse: float32 [5, 128, 128, 128], P(None, 'gx', 'gy'), may hold values from -6 to 6
- fine_density_state: float32 [512, 5, 16, 16, 128], P(('gx', 'gy')), may hold values from -6 to 6
- corners: int32 [512, 3], replicated, may hold values from -1 to 240, as said below
- ghost_source: int32 [512, 6], replicated, may hold values from -1 to 511, as said below
- courant: float32 [3, 5], replicated, may hold values from -0.3 to 0.3
- reaction: float32 [5, 5], replicated, may hold values from -1 to 1
Outputs:
- coarse_new: float32 [5, 128, 128, 128], P(None, 'gx', 'gy')
- fine_new: float32 [512, 5, 16, 16, 128], P(('gx', 'gy'))
Inputs may be any that keep to these rules, and one draw needn't show every extreme that they name: `corners`: row s is the lower fine corner of the box in slot s, slot s held by device s // 2 (device index gx * 16 + gy), or -1 -1 -1 for an empty slot. Corners are multiples of 16, 16 and 128; a box lies over the coarse columns of a device with the same gx index as the device holding its slot; no two boxes at one place; each gx index has 8 boxes; a device holds at most 2 boxes and some device of each gx index exactly 2. `ghost_source`: for faces west, east, south, north, bottom, top of the box in slot s: the slot of the box on the other side, or -1 where that place is not refined or lies outside the grid's bottom or top; all -1 for empty slots.
All inputs are finite; a program needn't handle non-finite values.
Results may differ from a plain program's by a relative error of at most 0.0003.
Values sent between devices are 32-bit elements; how exact they have to be, the bound alone decides.
No kernel may reach another device: no remote copies, remote signals or barrier semaphores. Data moves between devices by JAX's collectives and lax.ppermute only.
A program may use at most 192 MiB of HBM per device.

v0:
```python
import jax
import jax.numpy as jnp
from jax import lax
from jax.experimental import pallas as pl
from jax.experimental.pallas import tpu as pltpu
from jax.sharding import PartitionSpec as P

CHIP_OF = (0, 1, 2, 3, 7, 6, 5, 4)
SPECIES = 5
GX = 16
GY = 16
BOXES = 8
CHUNKS = 8
QUADS = 4
ROW_SLOTS = 32
FINE_ROWS = 160
PIECE_ROWS = 184
EDGE_ROWS = 80
EDGE_COARSE = 40
STRIDE = 16
LIST_STRIDE = 40
F32 = jnp.float32
SLOT, COL, HALF, WEST, EAST, SOUTH, NORTH, BOTTOM, TOP, OPEN_Z = range(10)
BESIDE = BOXES * STRIDE
OWN = BESIDE + 2 * GY
TABLE = OWN + 4
SHELL_ROWS = 80
PLANE_ROWS = 104
BACK_ROWS = 128

VMEM = pl.BlockSpec(memory_space=pltpu.VMEM)
SMEM = pl.BlockSpec(memory_space=pltpu.SMEM)
HBM = pl.BlockSpec(memory_space=pltpu.HBM)


def device_of(m, part, row):
    turned = (GY // 2) * (row % 2) if isinstance(row, int) else (GY // 2) * lax.rem(row, 2)
    place = 2 * CHIP_OF[m] + part + turned
    return place % GY if isinstance(row, int) else lax.rem(place, GY)


def chunk():
    turned = (GY // 2) * lax.rem(lax.axis_index("gx"), 2)
    j = lax.rem(lax.axis_index("gy") + turned, GY)
    q = j // 2
    return jnp.where(q < 4, q, 11 - q), lax.rem(j, 2)


def fill_table(corners, sources, table, listed, ranks):
    row = lax.axis_index("gx")
    m, part = chunk()
    groups = (row, lax.rem(row + jnp.where(part > 0, 1, GX - 1), GX))

    def scan(t, counts):
        new_counts = []
        for r in range(2):
            live = corners[0, groups[r] * ROW_SLOTS + t] >= 0
            listed[r * LIST_STRIDE + counts[r]] = t
            ranks[r * ROW_SLOTS + t] = counts[r]
            new_counts.append(counts[r] + jnp.where(live, 1, 0))
        return tuple(new_counts)

    lax.fori_loop(0, ROW_SLOTS, scan, (jnp.int32(0), jnp.int32(0)), unroll=True)

    def rank(r, source):
        found = ranks[r * ROW_SLOTS + lax.rem(jnp.maximum(source, 0), ROW_SLOTS)]
        return jnp.where(source >= 0, found, -1)

    for k in range(2 * GY):
        table[BESIDE + k] = -1
    for k in range(2):
        slot = row * ROW_SLOTS + 2 * lax.axis_index("gy") + k
        table[OWN + 2 * k] = jnp.where(corners[0, slot] >= 0, 1, 0)
        table[OWN + 2 * k + 1] = corners[2, slot] // 128
    face = jnp.where(part > 0, 0, 1)
    for i in range(BOXES):
        t = listed[i]
        slot = groups[0] * ROW_SLOTS + t
        south, north, bottom, top = [sources[f, slot] for f in range(2, 6)]
        beside = rank(1, sources[1 - face, slot])
        half = corners[2, slot] // 128
        base = STRIDE * i
        table[base + SLOT] = t
        table[base + COL] = corners[1, slot] // 16
        table[base + HALF] = half
        table[base + WEST] = jnp.where(part > 0, i, beside)
        table[base + EAST] = jnp.where(part > 0, beside, i)
        table[base + SOUTH] = rank(0, south)
        table[base + NORTH] = rank(0, north)
        table[base + BOTTOM] = jnp.where(m > 0, i, rank(0, bottom))
        table[base + TOP] = jnp.where(m < CHUNKS - 1, i, rank(0, top))
        table[base + OPEN_Z] = jnp.where(jnp.where(half > 0, bottom, top) < 0, 1, 0)
        other = groups[1] * ROW_SLOTS + listed[LIST_STRIDE + i]
        spot = corners[1, other] // 16 * 2 + corners[2, other] // 128
        table[BESIDE + spot] = jnp.where(sources[face, other] < 0, i, -1)


def pack_kernel(
    corners_in, sources_in, coarse_in, fine_in, out, table, coarse, fine, loaded, listed, ranks, corners, sources,
    around,
):
    row, column = lax.axis_index("gx"), lax.axis_index("gy")
    blocks = [(k, s) for k in range(2) for s in range(SPECIES)]
    loads = [pltpu.make_async_copy(fine_in.at[k, s], fine.at[k, s], loaded.at[n]) for n, (k, s) in enumerate(blocks)]
    loads.append(pltpu.make_async_copy(coarse_in, coarse, loaded.at[len(blocks)]))
    integers = (
        pltpu.make_async_copy(corners_in, corners, loaded.at[len(blocks) + 1]),
        pltpu.make_async_copy(sources_in, sources, loaded.at[len(blocks) + 2]),
    )
    for load in (*integers, *loads):
        load.start()
    for load in (*integers, *loads):
        load.wait()
    fill_table(corners, sources, table, listed, ranks)
    for n, (k, s) in enumerate(blocks):
        turned = fine[k, s].reshape(256, 128).T
        at = (k * SPECIES + s) * 16
        for m in range(CHUNKS):
            for part in range(2):
                block = turned[16 * m : 16 * m + 16, 128 * part : 128 * part + 128]
                out[device_of(m, part, row), at : at + 16, :] = block
    for p in range(3):
        at = FINE_ROWS + 8 * p
        for part in range(2):
            blocks = []
            for s in (2 * p, 2 * p + 1):
                block = coarse[min(s, 4), 4 * part : 4 * part + 4].reshape(32, 128)
                blocks += [block, pltpu.roll(block, 64, 1)]
            for n, block in enumerate(blocks):
                around[pl.ds(pl.multiple_of(32 * lax.rem(column + n, 4), 32), 32), :] = block
            turned = around[...].T
            for m in range(CHUNKS):
                out[device_of(m, part, row), at : at + 8, :] = turned[8 * m : 8 * m + 8]


def unpack_kernel(table, received, interior, coarse_out, fine_out, coarse, fine, stored, around, shells, planes):
    row, column = lax.axis_index("gx"), lax.axis_index("gy")
    rows, lanes = iotas()
    stores = []

    def send(source, target):
        stores.append(pltpu.make_async_copy(source, target, stored.at[len(stores)]))
        stores[-1].start()

    live = [table[OWN + 2 * k] > 0 for k in range(2)]
    high = [table[OWN + 2 * k + 1] > 0 for k in range(2)]
    in_plane = [jnp.where(high[k], lanes, 127 - lanes) < 2 for k in range(2)]
    for part in range(2):
        parts = []
        for k in range(2):
            source = jnp.where(high[k], device_of(0, part, row), device_of(CHUNKS - 1, part, row))
            parts.append(received[source, PLANE_ROWS + 10 * k : PLANE_ROWS + 10 * k + 10, :])
        planes[part] = jnp.concatenate([*parts, jnp.zeros((108, 128), F32)]).T
    for s in range(SPECIES):
        for part in range(2):
            pieces = [received[device_of(m, part, row), 16 * s : 16 * s + 16, :] for m in range(CHUNKS)]
            shells[part] = jnp.concatenate(pieces).T
        for k in range(2):
            shift = lax.rem(jnp.where(high[k], 128, 254) - (10 * k + 2 * s), 128)
            for x in range(16):
                part, at_x = x // 8, x % 8
                depth = at_x if part == 0 else 7 - at_x
                if depth < 2:
                    at = 64 * k + 16 * depth
                    tiles = [shells[part, at + 8 * j : at + 8 * j + 8, :] for j in range(2)]
                else:
                    at = 64 * k + 32 + 8 * ((depth - 2) // 2)
                    tile = shells[part, at : at + 8, :]
                    sides = (tile, tile) if depth % 2 == 0 else (turn(tile, -2, 0), turn(tile, 2, 0))
                    tiles = []
                    for j in range(2):
                        at = 16 * at_x + 8 * j
                        plane = pltpu.roll(planes[part, at : at + 8, :], shift, 1)
                        inner = jnp.where(in_plane[k], plane, interior[k, s, x, 8 * j : 8 * j + 8, :])
                        tiles.append(jnp.where(rows >= 6 if j else rows < 2, sides[j], inner))
                for j in range(2):
                    fine[k, s, x, 8 * j : 8 * j + 8, :] = jnp.where(live[k], tiles[j], 0.0)
            send(fine.at[k, s], fine_out.at[k, s])
    left = lax.broadcasted_iota(jnp.int32, (32, 128), 1) < 64
    for p in range(3):
        at = SHELL_ROWS + 8 * p
        pieces = [received[device_of(m, part, row), at : at + 8, :] for part in range(2) for m in range(CHUNKS)]
        around[...] = jnp.concatenate(pieces).T
        for s in range(2 * p, min(2 * p + 2, SPECIES)):
            low, high = [
                around[pl.ds(pl.multiple_of(32 * lax.rem(column + 2 * (s - 2 * p) + h, 4), 32), 32), :] for h in range(2)
            ]
            coarse[s, 0:4] = jnp.where(left, low, pltpu.roll(high, 64, 1)).reshape(4, 8, 128)
            coarse[s, 4:8] = jnp.where(left, pltpu.roll(low, 64, 1), high).reshape(4, 8, 128)
    send(coarse, coarse_out)
    for store in stores:
        store.wait()


def interior_kernel(courant, reaction, fine, out, between):
    rows, lanes = iotas()
    goes_up, size = signs_of(courant)
    weights = weights_of(size, reaction, 0.5)

    def step(load, store, first, last):
        def plane(x, carry):
            values = [[load(s, x, j) for s in range(SPECIES)] for j in range(2)]
            for s in range(SPECIES):
                up_x, up_y, up_z = [goes_up[d][s] for d in range(3)]
                before = x + jnp.where(up_x, -1, 1)
                low, high = [pltpu.roll(values[j][s], jnp.where(up_y, 1, 7), 0) for j in range(2)]
                from_y = (
                    jnp.where((rows == 7) & jnp.logical_not(up_y), high, low),
                    jnp.where((rows == 0) & up_y, low, high),
                )
                for j in range(2):
                    from_z = pltpu.roll(values[j][s], jnp.where(up_z, 1, 127), 1)
                    from_z = jnp.where(lanes == jnp.where(up_z, 0, 127), 0.0, from_z)
                    upwind = (load(s, before, j), from_y[j], from_z)
                    store(s, x, j, moved(values[j], upwind, size, weights, s))
            return carry

        lax.fori_loop(first, last, plane, 0, unroll=2)

    for k in range(2):

        def put(ref):
            def store(s, x, j, tile):
                ref[s, x, 8 * j : 8 * j + 8, :] = tile

            return store

        def get(ref):
            return lambda s, x, j: ref[s, x, 8 * j : 8 * j + 8, :]

        step(get(fine.at[k]), put(between), 1, 15)
        step(get(between), put(out.at[k]), 2, 14)


def iotas():
    return lax.broadcasted_iota(jnp.int32, (8, 128), 0), lax.broadcasted_iota(jnp.int32, (8, 128), 1)


def take(tile, index, axis):
    return jnp.take_along_axis(tile, index, axis=axis, mode="promise_in_bounds")


def turn(tile, shift, axis):
    return pltpu.roll(tile, shift % tile.shape[axis], axis)


def line(ref, index):
    return jnp.broadcast_to(ref[pl.ds(index, 1), :], (8, 128))


def edges(fine, coarse, up_out, down_out, outer_out, inner_out):
    _, lanes = iotas()
    _, part = chunk()
    last = part > 0
    for s in range(SPECIES):
        up_out[8 * s : 8 * s + 8, :] = fine[1][:, s, 7, :]
        down_out[8 * s : 8 * s + 8, :] = fine[0][:, s, 0, :]
        for h in range(2):
            at = EDGE_COARSE + (2 * s + h) * QUADS
            up_out[at : at + QUADS, :] = coarse[:, s, h, 7, :]
            down_out[at : at + QUADS, :] = coarse[:, s, h, 0, :]
        for r in range(2):
            low = high = coarse_low = coarse_high = jnp.zeros((8, 128), F32)
            for i in range(BOXES):
                here = lanes // 16 == i
                low = jnp.where(here, turn(fine[r][i, s], 16 * i, 1), low)
                high = jnp.where(here, turn(fine[r][i, s], 16 * i + 16, 1), high)
            for q in range(QUADS):
                here = lax.rem(lanes // 8, 4) == q
                coarse_low = jnp.where(here, turn(coarse[q, s, r], 8 * q, 1), coarse_low)
                coarse_high = jnp.where(here, turn(coarse[q, s, r], 8 * q - 24, 1), coarse_high)
            outer_out[0, s, r] = jnp.where(last, high, low)
            inner_out[0, s, r] = jnp.where(last, low, high)
            outer_out[1, s, r] = jnp.where(last, coarse_high, coarse_low)
            inner_out[1, s, r] = jnp.where(last, coarse_low, coarse_high)


def compact_kernel(table, received, fine0, fine1, coarse, up_out, down_out, outer_out, inner_out):
    _, lanes = iotas()
    for i in range(BOXES):
        t = table[STRIDE * i + SLOT]
        start = pl.multiple_of(lax.rem(t, 2) * 80, 8)
        box = received[t // 2, pl.ds(start, 80), :].reshape(SPECIES, 2, 8, 128)
        fine0[i] = box[:, 0]
        fine1[i] = box[:, 1]
    for q in range(QUADS):
        for p in range(3):
            at = FINE_ROWS + 8 * p
            tiles = [received[4 * q + o, at : at + 8, :] for o in range(4)]
            for k in range(4 if p < 2 else 2):
                tile = tiles[0]
                for o in range(1, 4):
                    tile = jnp.where(lanes // 32 == (o + k) % 4, tiles[o], tile)
                coarse[q, 2 * p + k // 2, k % 2] = turn(tile, -32 * k, 1)
    edges((fine0, fine1), coarse, up_out, down_out, outer_out, inner_out)


def signs_of(courant):
    goes_up = [[courant[d, s] >= 0.0 for s in range(SPECIES)] for d in range(3)]
    size = [[jnp.abs(courant[d, s]) for s in range(SPECIES)] for d in range(3)]
    return goes_up, size


def weights_of(size, reaction, factor):
    weights = [[factor * reaction[s, e] for e in range(SPECIES)] for s in range(SPECIES)]
    for s in range(SPECIES):
        weights[s][s] = weights[s][s] + (1.0 - size[0][s] - size[1][s] - size[2][s])
    return weights


def moved(values, upwind, size, weights, s):
    total = weights[s][0] * values[0]
    for e in range(1, SPECIES):
        total = total + weights[s][e] * values[e]
    for d in range(3):
        total = total + size[d][s] * upwind[d]
    return total


def ends(table, below, above, ghosts):
    _, lanes = iotas()
    m, _ = chunk()
    ghosts[:EDGE_COARSE, :] = below[:EDGE_COARSE, :]
    ghosts[EDGE_COARSE:, :] = above[:EDGE_COARSE, :]

    def replace(side, source, name, high):
        for i in range(BOXES):
            col, half, found = [table[STRIDE * i + f] for f in (COL, HALF, name)]
            inside = 32 * lax.rem(col, 4) + 8 * (lanes // 32) + lax.rem(lanes, 16) // 2
            for s in range(SPECIES):
                other = take(line(source, EDGE_COARSE + (2 * s + side) * QUADS + col // 4), inside, 1)
                other = jnp.where(half == high, other, 0.0)
                ghost = jnp.where(found >= 0, line(source, 8 * s + jnp.maximum(found, 0)), other)
                at = EDGE_COARSE * side + 8 * s + i
                ghosts[at : at + 1, :] = ghost[:1]

    @pl.when(m == 0)
    def _():
        replace(0, below, BOTTOM, 1)

    @pl.when(m == CHUNKS - 1)
    def _():
        replace(1, above, TOP, 0)


def fine_step(i, table, fine, coarse, ghosts, sides, goes_up, size, weights, write):
    rows, lanes = iotas()
    field = lambda f: table[STRIDE * i + f]
    col, half = field(COL), field(HALF)
    lower_col, upper_col = lax.rem(col + GY - 1, GY), lax.rem(col + 1, GY)
    y = lax.rem(lanes, 16)
    found = [field(f) for f in (WEST, EAST, SOUTH, NORTH)]
    there = [source >= 0 for source in found]
    at = [jnp.maximum(source, 0) for source in found]
    beside = 32 * lax.rem(col, 4) + 8 * (col // 4) + y // 2
    lane_x = [jnp.where(there[f], 16 * at[f] + y, beside) for f in range(2)]
    own_x, line_x = lanes - y, 8 * (lanes // 32)
    lane_y = [
        jnp.where(there[2], own_x + 15, 32 * lax.rem(lower_col, 4) + line_x + 7),
        jnp.where(there[3], own_x, 32 * lax.rem(upper_col, 4) + line_x),
    ]
    row_of = [[jnp.where(is_there, rows, 4 * r + rows // 2) for is_there in there] for r in range(2)]
    kind = [jnp.where(is_there, 0, 1) for is_there in there]
    values = [[fine[r][i, s] for s in range(SPECIES)] for r in range(2)]
    for s in range(SPECIES):
        up_x, up_y, up_z = [goes_up[d][s] for d in range(3)]
        shift_x, edge_x = jnp.where(up_x, 16, 112), lanes // 16 == jnp.where(up_x, 0, 7)
        shift_y, edge_y = jnp.where(up_y, 1, 127), y == jnp.where(up_y, 0, 15)
        shift_z, edge_z = jnp.where(up_z, 1, 7), rows == jnp.where(up_z, 0, 7)
        is_there = jnp.where(up_y, found[2], found[3]) >= 0
        box_y = jnp.where(up_y, at[2], at[3])
        quad_y = jnp.where(up_y, lower_col, upper_col) // 4
        coarse_y = coarse[quad_y, s, half]
        index_x = jnp.where(up_x, lane_x[0], lane_x[1])
        index_y = jnp.where(up_y, lane_y[0], lane_y[1])

        low, high = values[0][s], values[1][s]
        first = pltpu.roll(jnp.where(up_z, low, high), shift_z, 0)
        second = pltpu.roll(jnp.where(up_z, high, low), shift_z, 0)
        second = jnp.where(edge_z, first, second)
        first = jnp.where(edge_z, line(ghosts, jnp.where(up_z, 0, EDGE_COARSE) + 8 * s + i), first)
        from_z = (jnp.where(up_z, first, second), jnp.where(up_z, second, first))

        for r in range(2):
            value = values[r][s]
            west = sides(0, kind[0], s, jnp.where(there[0], r, half))
            east = sides(1, kind[1], s, jnp.where(there[1], r, half))
            ghost = take(jnp.where(up_x, west, east), jnp.where(up_x, row_of[r][0], row_of[r][1]), 0)
            ghost = take(ghost, index_x, 1)
            from_x = jnp.where(edge_x, ghost, pltpu.roll(value, shift_x, 1))
            ghost = take(
                jnp.where(is_there, fine[r][box_y, s], coarse_y), jnp.where(up_y, row_of[r][2], row_of[r][3]), 0
            )
            ghost = take(ghost, index_y, 1)
            from_y = jnp.where(edge_y, ghost, pltpu.roll(value, shift_y, 1))
            write(r, s, moved(values[r], (from_x, from_y, from_z[r]), size, weights, s))


def sides_of(outer, inner):
    _, part = chunk()

    def pick(side, kind, s, at):
        one, other = outer[kind, s, at], inner[kind, s, at]
        return jnp.where(part == side, one, other)

    return pick


def first_kernel(
    table, courant, reaction, fine0, fine1, coarse, below, above, outer, inner,
    new0, new1, middle, provisional, up_out, down_out, outer_out, inner_out, ghosts,
):
    rows, lanes = iotas()
    m, _ = chunk()
    goes_up, size = signs_of(courant)
    weights = weights_of(size, reaction, 1.0)
    x = lax.rem(lanes // 8, 4)
    y = lax.rem(lanes, 8)
    sides = sides_of(outer, inner)
    ends(table, below, above, ghosts)

    def coarse_quad(q, carry):
        before, after = lax.rem(q + QUADS - 1, QUADS), lax.rem(q + 1, QUADS)
        values = [[coarse[q, s, h] for s in range(SPECIES)] for h in range(2)]
        column = 32 * (lanes // 32) + 8 * q + y
        for s in range(SPECIES):
            up_x, up_y, up_z = [goes_up[d][s] for d in range(3)]
            at = [EDGE_COARSE + (2 * s + h) * QUADS + q for h in range(2)]
            lows, highs = [line(below, k) for k in at], [line(above, k) for k in at]
            bottoms = (jnp.where(m > 0, lows[0], 0.0), jnp.where(m > 0, lows[1], lows[0]))
            tops = (
                jnp.where(m < CHUNKS - 1, highs[0], highs[1]),
                jnp.where(m < CHUNKS - 1, highs[1], 0.0),
            )
            for h in range(2):
                value = values[h][s]
                ghost = take(jnp.where(up_x, sides(0, 1, s, h), sides(1, 1, s, h)), column, 1)
                from_x = pltpu.roll(value, jnp.where(up_x, 8, 120), 1)
                from_x = jnp.where(x == jnp.where(up_x, 0, 3), ghost, from_x)

                beside = coarse[jnp.where(up_y, before, after), s, h]
                ghost = jnp.where(lanes // 32 == jnp.where(up_y, 3, 0), beside, value)
                ghost = pltpu.roll(ghost, jnp.where(up_y, 25, 103), 1)
                from_y = pltpu.roll(value, jnp.where(up_y, 1, 127), 1)
                from_y = jnp.where(y == jnp.where(up_y, 0, 7), ghost, from_y)

                ghost = jnp.where(up_z, bottoms[h], tops[h])
                from_z = pltpu.roll(value, jnp.where(up_z, 1, 7), 0)
                from_z = jnp.where(rows == jnp.where(up_z, 0, 7), ghost, from_z)

                result = moved(values[h], (from_x, from_y, from_z), size, weights, s)
                provisional[q, s, h] = result
                middle[q, s, h] = 0.5 * (value + result)
        return carry

    lax.fori_loop(0, QUADS, coarse_quad, 0, unroll=4)
    new = (new0, new1)
    weights = weights_of(size, reaction, 0.5)

    def box(i, carry):
        def write(r, s, result):
            new[r][i, s] = result

        fine_step(i, table, (fine0, fine1), coarse, ghosts, sides, goes_up, size, weights, write)
        return carry

    lax.fori_loop(0, BOXES, box, 0, unroll=8)
    edges(new, middle, up_out, down_out, outer_out, inner_out)


def tools_of(courant, coarse_new, folded0, folded1):
    up = [[jnp.maximum(courant[d, s], 0.0) for s in range(SPECIES)] for d in range(3)]
    down = [[jnp.minimum(courant[d, s], 0.0) for s in range(SPECIES)] for d in range(3)]
    taken = lax.broadcasted_iota(jnp.int32, (128, 128), 0)
    given = lax.broadcasted_iota(jnp.int32, (128, 128), 1)
    given_y, fine_y = lax.rem(given, 8), lax.rem(taken, 16)
    same_x = lax.rem(given // 8, 4) == taken // 32

    def summing(rule):
        return jnp.where(same_x & rule(given_y, fine_y), 1.0, 0.0).astype(F32)

    def product(values, matrix):
        return jnp.dot(values, matrix, precision=lax.Precision.HIGHEST, preferred_element_type=F32)

    def fold(tiles, matrix):
        for refs, folded in zip(tiles, (folded0, folded1)):
            pairs = sum(
                ref.reshape(BOXES * SPECIES * 8, 128)[pl.ds(odd, BOXES * SPECIES * 4, stride=2), :]
                for ref in refs
                for odd in range(2)
            )
            folded[...] = product(pairs, matrix)

    def folded_tile(i, s):
        at = pl.ds((i * SPECIES + s) * 4, 4)
        return jnp.concatenate([folded0[at, :], folded1[at, :]])

    def add(q, s, h, where, change):
        coarse_new[q, s, h] = coarse_new[q, s, h] + jnp.where(where, change, 0.0)

    def change_of(here, across, both, beside, rate_out, rate_in, sign):
        return sign * (rate_out * (here - 0.5 * both) + rate_in * (across - 0.125 * beside))

    return up, down, summing, product, fold, folded_tile, add, change_of


def beside_kernel(table, courant, old0, old1, coarse, fine0, fine1, middle, provisional, coarse_new, folded0, folded1):
    _, lanes = iotas()
    y = lax.rem(lanes, 8)
    group = lanes // 32
    up, down, summing, _, fold, folded_tile, add, change_of = tools_of(courant, coarse_new, folded0, folded1)
    coarse_new[...] = provisional[...]

    def rule(given_y, fine_y):
        return ((fine_y == 0) & (given_y == 7)) | ((fine_y == 15) & (given_y == 0))

    fold(((old0, fine0), (old1, fine1)), summing(rule))

    def open_y(i, carry):
        col, half, south, north = [table[STRIDE * i + f] for f in (COL, HALF, SOUTH, NORTH)]
        south_col, north_col = lax.rem(col + GY - 1, GY), lax.rem(col + 1, GY)
        south_quad, north_quad = south_col // 4, north_col // 4
        at_south = (group == lax.rem(south_col, 4)) & (y == 7) & (south < 0)
        at_north = (group == lax.rem(north_col, 4)) & (y == 0) & (north < 0)
        for s in range(SPECIES):
            beside = folded_tile(i, s)
            tile = coarse[col // 4, s, half]
            here = coarse[south_quad, s, half]
            both = here + middle[south_quad, s, half]
            change = change_of(here, turn(tile, -25, 1), both, beside, up[1][s], down[1][s], 1.0)
            add(south_quad, s, half, at_south, change)
            here = coarse[north_quad, s, half]
            both = here + middle[north_quad, s, half]
            change = change_of(here, turn(tile, 25, 1), both, beside, down[1][s], up[1][s], -1.0)
            add(north_quad, s, half, at_north, change)
        return carry

    lax.fori_loop(0, BOXES, open_y, 0, unroll=8)


def second_kernel(
    table, courant, reaction, old0, old1, coarse, old_below, old_above, old_outer, old_inner,
    fine0, fine1, middle, below, above, outer, inner, corrected, out,
    coarse_new, ghosts, result0, result1, folded0, folded1,
):
    rows, lanes = iotas()
    m, part = chunk()
    goes_up, size = signs_of(courant)
    weights = weights_of(size, reaction, 0.5)
    up, down, summing, product, fold, folded_tile, add, change_of = tools_of(courant, coarse_new, folded0, folded1)
    x = lax.rem(lanes // 8, 4)
    y = lax.rem(lanes, 8)
    group = lanes // 32
    ends(table, below, above, ghosts)
    coarse_new[...] = corrected[...]

    sides = sides_of(outer, inner)

    def box_step(i, carry):
        def write(r, s, result):
            (result0, result1)[r][i, s] = result

        fine_step(i, table, (fine0, fine1), middle, ghosts, sides, goes_up, size, weights, write)
        return carry

    lax.fori_loop(0, BOXES, box_step, 0, unroll=8)

    place = lax.rem(lanes, 64)
    rest = jnp.maximum(place - 32, 0)
    slot = lax.rem(rest, 8)
    is_second = (slot >= 2) & (slot < 6)
    depth = jnp.where(place < 32, place // 16, 2 + 2 * (rest // 8) + jnp.where(is_second, 1, 0))
    depth = jnp.minimum(depth, 7)
    rest_y = jnp.where(is_second, slot - 2, slot)
    rest_y = jnp.where(slot >= 4, jnp.where(is_second, slot + 10, slot + 8), rest_y)
    shell_y = jnp.where(place < 32, lax.rem(place, 16), rest_y)
    shell_index = 16 * jnp.where(part > 0, 7 - depth, depth) + shell_y

    def pack_box(i, carry):
        t = table[STRIDE * i + SLOT]
        k = lax.rem(t, 2)
        mine = lanes // 64 == k
        for s in range(SPECIES):
            for r, result in enumerate((result0, result1)):
                at = (2 * s + r) * 8
                packed = take(result[i, s], shell_index, 1)
                out[t // 2, at : at + 8, :] = jnp.where(mine, packed, out[t // 2, at : at + 8, :])
            plane = jnp.where(m == 0, result0[i, s, 0:2, :], result1[i, s, 6:8, :])
            out[t // 2, pl.ds(PLANE_ROWS + 10 * k + 2 * s, 2), :] = plane
        return carry

    lax.fori_loop(0, BOXES, pack_box, 0, unroll=4)
    mean_matrix = summing(lambda given_y, fine_y: fine_y // 2 == given_y)

    def open_z(high, row, source, old_source, rate_out, rate_in, sign):
        folded0[:EDGE_COARSE, :] = product(source[:EDGE_COARSE, :] + old_source[:EDGE_COARSE, :], mean_matrix)
        for i in range(BOXES):
            col, half, is_open = [table[STRIDE * i + f] for f in (COL, HALF, OPEN_Z)]
            q = col // 4
            where = (rows == row) & (group == lax.rem(col, 4)) & (half == high) & (is_open > 0)
            for s in range(SPECIES):
                beside = jnp.broadcast_to(folded0[8 * s + i : 8 * s + i + 1, :], (8, 128))
                here = coarse[q, s, 1 - high]
                across = line(old_source, EDGE_COARSE + (2 * s + high) * QUADS + q)
                both = here + middle[q, s, 1 - high]
                change = change_of(here, across, both, beside, rate_out[s], rate_in[s], sign)
                add(q, s, 1 - high, where, change)

    @pl.when(m == CHUNKS - 1)
    def _():
        open_z(1, 7, above, old_above, up[2], down[2], 1.0)

    @pl.when(m == 0)
    def _():
        open_z(0, 0, below, old_below, down[2], up[2], -1.0)

    row_index = 2 * lax.rem(rows, 4)
    last = part > 0
    edge = jnp.where(last, 3, 0)
    sign = jnp.where(last, 1.0, -1.0)
    sums = []
    for s in range(SPECIES):
        totals = [old_outer[0, s, r] + outer[0, s, r] for r in range(2)]
        totals = [take(total + turn(total, -1, 0), row_index, 0) for total in totals]
        total = jnp.where(rows < 4, totals[0], totals[1])
        sums.append(total + turn(total, -1, 1))

    def open_x(q, carry):
        column = 32 * group + 8 * q + y
        for h in range(2):
            box = table[BESIDE + 2 * (4 * q) + h]
            for o in range(1, 4):
                box = jnp.where(group == o, table[BESIDE + 2 * (4 * q + o) + h], box)
            where = (box >= 0) & (x == edge)
            index = 16 * jnp.maximum(box, 0) + 2 * y
            for s in range(SPECIES):
                rate_out = jnp.where(last, up[0][s], down[0][s])
                rate_in = jnp.where(last, down[0][s], up[0][s])
                here = coarse[q, s, h]
                across = take(old_outer[1, s, h], column, 1)
                both = here + middle[q, s, h]
                beside = take(sums[s], index, 1)
                add(q, s, h, where, change_of(here, across, both, beside, rate_out, rate_in, sign))
        return carry

    lax.fori_loop(0, QUADS, open_x, 0, unroll=4)
    fold(((result0,), (result1,)), mean_matrix)

    def cover(i, carry):
        col, half = [table[STRIDE * i + f] for f in (COL, HALF)]
        q = col // 4
        where = group == lax.rem(col, 4)
        for s in range(SPECIES):
            coarse_new[q, s, half] = jnp.where(where, 0.125 * folded_tile(i, s), coarse_new[q, s, half])
        return carry

    lax.fori_loop(0, BOXES, cover, 0, unroll=8)
    for q in range(QUADS):
        for p in range(3):
            at = SHELL_ROWS + 8 * p
            tiles = [turn(coarse_new[q, 2 * p + k // 2, k % 2], 32 * k, 1) for k in range(4 if p < 2 else 2)]
            for o in range(4):
                tile = tiles[0]
                for k in range(1, len(tiles)):
                    tile = jnp.where(group == (o + k) % 4, tiles[k], tile)
                out[4 * q + o, at : at + 8, :] = tile


def call(kernel, out_shape, operands, smem, scratch=(), in_spec=VMEM, out_spec=VMEM):
    many = isinstance(out_shape, (list, tuple))
    specs = [out_spec] * len(out_shape) if many and not isinstance(out_spec, list) else out_spec
    return pl.pallas_call(
        kernel,
        out_shape=out_shape,
        in_specs=[SMEM] * smem + [in_spec] * (len(operands) - smem),
        out_specs=specs,
        scratch_shapes=list(scratch),
        compiler_params=pltpu.CompilerParams(vmem_limit_bytes=40 * 1024 * 1024),
    )(*operands)


def exchange(up_edge, down_edge, outer_edge, inner_edge):
    device = lambda g, m, part: g % GX * GY + device_of(m % CHUNKS, part, g % GX)
    all_of = [(g, m, part) for g in range(GX) for m in range(CHUNKS) for part in range(2)]
    axes = ("gx", "gy")
    send = lambda value, target: lax.ppermute(value, axes, [(device(*d), device(*target(*d))) for d in all_of])
    outer = send(outer_edge, lambda g, m, part: (g + 2 * part - 1, m, 1 - part))
    below = send(up_edge, lambda g, m, part: (g, m + 1, part))
    above = send(down_edge, lambda g, m, part: (g, m - 1, part))
    inner = send(inner_edge, lambda g, m, part: (g, m, 1 - part))
    return below, above, outer, inner


def spread(pieces):
    return lax.all_to_all(pieces, "gy", 0, 0, tiled=True)


def shards(coarse, fine, corners, ghost_source, courant, reaction):
    shape = lambda *dims: jax.ShapeDtypeStruct(dims, F32)
    pieces = shape(GY, PIECE_ROWS, 128)
    boxes = shape(BOXES, SPECIES, 8, 128)
    grid = shape(QUADS, SPECIES, 2, 8, 128)
    sent = (shape(EDGE_ROWS, 128),) * 2 + (shape(2, SPECIES, 2, 8, 128),) * 2
    whole = (pltpu.VMEM(coarse.shape, F32), pltpu.VMEM(fine.shape, F32))
    copies = pltpu.SemaphoreType.DMA((2 * SPECIES + 1,))
    integers = lambda *dims: pltpu.SMEM(dims, jnp.int32)
    placed = [pltpu.with_memory_space_constraint(value, pltpu.HBM) for value in (corners.T, ghost_source.T, coarse, fine)]
    sending, table = call(
        pack_kernel,
        [pltpu.VMEM(pieces.shape, F32), jax.ShapeDtypeStruct((TABLE,), jnp.int32)],
        placed,
        0,
        (
            *whole,
            pltpu.SemaphoreType.DMA((2 * SPECIES + 3,)),
            integers(2 * LIST_STRIDE),
            integers(2 * ROW_SLOTS),
            integers(3, 512),
            integers(6, 512),
            pltpu.VMEM((128, 128), F32),
        ),
        HBM,
        [VMEM, SMEM],
    )
    received = spread(sending)
    fine0, fine1, middle, *sending = call(compact_kernel, (boxes, boxes, grid) + sent, (table, received), 1)
    old = (fine0, fine1, middle, *exchange(*sending))
    between = (pltpu.VMEM(fine.shape[1:], F32),)
    held, _ = lax.optimization_barrier((fine, old[0]))
    interior = call(interior_kernel, shape(*fine.shape), (courant, reaction, held), 2, between)
    interior, *old = lax.optimization_barrier((interior, *old))
    old = tuple(old)
    ghosts = pltpu.VMEM((EDGE_ROWS, 128), F32)
    new0, new1, middle, provisional, *sending = call(
        first_kernel, (boxes, boxes, grid, grid) + sent, (table, courant, reaction) + old, 3, (ghosts,)
    )
    new = (new0, new1, middle, *exchange(*sending))
    folded = (pltpu.VMEM((BOXES * SPECIES * 4, 128), F32),) * 2
    operands = (table, courant) + old[:3] + new[:3] + (provisional,)
    corrected = call(beside_kernel, grid, operands, 2, folded)
    scratch = (
        pltpu.VMEM(grid.shape, F32),
        ghosts,
        pltpu.VMEM(boxes.shape, F32),
        pltpu.VMEM(boxes.shape, F32),
        *folded,
    )
    back = call(
        second_kernel, shape(GY, BACK_ROWS, 128), (table, courant, reaction) + old + new + (corrected,), 3, scratch
    )
    outputs = (shape(*coarse.shape), shape(*fine.shape))
    scratch = (
        *whole,
        copies,
        pltpu.VMEM((128, 128), F32),
        pltpu.VMEM((2, 128, 128), F32),
        pltpu.VMEM((2, 128, 128), F32),
    )
    return call(unpack_kernel, outputs, (table, spread(back), interior), 1, scratch, VMEM, HBM)


def solution(mesh):
    fine_spec = P(("gx", "gy"), None, None, None, None)
    coarse_spec = P(None, "gx", "gy", None)
    return jax.shard_map(
        shards,
        mesh=mesh,
        in_specs=(coarse_spec, fine_spec, P(), P(), P(), P()),
        out_specs=(coarse_spec, fine_spec),
        check_vma=False,
    )
```

profile of v0, /device:TPU:1, one launch (start us, length us, event | category | flops | bytes accessed | tf_op | source)
XLA Modules:
  0.0 77.0 jit_solution(8632271283755950180)
XLA Ops:
  0.6 3.0 %shard_map.77 = (f32[16,184,128]{2,1,0:T(8,128)S(1)}, s32[164]{0:T(256)S(1)}) custom-call(s32[3,512]{1,0:T(4,128)} %bitcast.3, s32[6,512]{1,0:T(8,128)} %bitcast.2, f32[5,8,8,128]{3,2,1,0:T(8,128)} %coarse_in.1, f32[2,5,16,16,128]{4,3,2,1,0:T(8,128)} %fine), custom_call_target="tpu_custom_call" | custom-call | tf_op jit(solution)/shard_map/pallas_call | solution.py:672
  3.6 27.0 %all_to_all.10.received = f32[16,184,128]{2,1,0:T(8,128)S(1)} all-to-all(f32[16,184,128]{2,1,0:T(8,128)S(1)} %get-tuple-element.29), channel_id=1, replica_groups=mesh['gx'=16,'gy'=16] {'gy'}, dimensions={0} | all-to-all | bytes 3014656 | tf_op jit(solution)/shard_map/all_to_all | solution.py:695
  30.6 0.0 copy-start
  30.6 0.0 copy-start.1
  30.6 0.0 copy-start.2
  30.6 0.9 %shard_map.78 = (f32[8,5,8,128]{3,2,1,0:T(8,128)S(1)}, f32[8,5,8,128]{3,2,1,0:T(8,128)S(1)}, f32[4,5,2,8,128]{4,3,2,1,0:T(8,128)S(1)}, f32[80,128]{1,0:T(8,128)S...) custom-call(s32[164]{0:T(256)S(1)} %get-tuple-element.28.table, ...), custom_call_target="tpu_custom_call" | custom-call | tf_op jit(solution)/shard_map/pallas_call | solution.py:672
  31.6 2.7 %collective-permute-start.2 = (f32[2,5,2,8,128]{4,3,2,1,0:T(8,128)S(1)}, f32[2,5,2,8,128]{4,3,2,1,0:T(8,128)S(1)}, u32[]{:S(2)}, u32[]{:S(2)}) collective-permute-start(f32[2,5,2,8,128]{4,3,2,1,0:T(8,128)S(1)} %get-tuple-element.36), channel_id=1, source_target_pairs={{0,249},{1,24},{2,251},{3,26},{4,253},{5,28},{6,255},{7,30},{14,24... | collective-permute-start | bytes 245768 | tf_op jit(solution)/shard_map/ppermute | solution.py:686
  34.2 5.2 %collective-permute-start.3 = (f32[2,5,2,8,128]{4,3,2,1,0:T(8,128)S(1)}, f32[2,5,2,8,128]{4,3,2,1,0:T(8,128)S(1)}, u32[]{:S(2)}, u32[]{:S(2)}) collective-permute-start(f32[2,5,2,8,128]{4,3,2,1,0:T(8,128)S(1)} %get-tuple-element.37), channel_id=1, source_target_pairs={{0,1},{1,0},{2,3},{3,2},{4,5},{5,4},{6,7},{7,6},{14,15},{15,14},{1... | collective-permute-start | bytes 245768 | tf_op jit(solution)/shard_map/ppermute | solution.py:686
  39.4 0.2 collective-permute-start
  39.6 1.3 %collective-permute-start.1 = (f32[80,128]{1,0:T(8,128)S(1)}, f32[80,128]{1,0:T(8,128)S(1)}, u32[]{:S(2)}, u32[]{:S(2)}) collective-permute-start(f32[80,128]{1,0:T(8,128)S(1)} %get-tuple-element.35), channel_id=1, source_target_pairs={{0,8},{1,9},{2,0},{3,1},{4,2},{5,3},{6,4},{7,5},{14,6},{15,7},{12,... | collective-permute-start | bytes 122888 | tf_op jit(solution)/shard_map/ppermute | solution.py:686
  40.9 0.0 copy-done
  40.9 0.0 copy-done.1
  40.9 0.0 copy-done.2
  40.9 3.2 %shard_map.79.interior = f32[2,5,16,16,128]{4,3,2,1,0:T(8,128)S(1)} custom-call(f32[3,5]{1,0:T(4,128)S(1)} %copy-done.2, f32[5,5]{1,0:T(8,128)S(1)} %copy-done.1, f32[2,5,16,16,128]{4,3,2,1,0:T(8,128)S(1)} %copy-done), custom_call_target="tpu_custom_call" | custom-call | tf_op jit(solution)/shard_map/pallas_call | solution.py:672
  44.0 0.0 collective-permute-done.below.old_below
  44.1 0.0 collective-permute-done.1.above.old_above
  44.1 0.0 collective-permute-done.2.outer.old_outer
  44.1 0.0 collective-permute-done.3.inner.old_inner
  44.1 2.2 %shard_map.80 = (f32[8,5,8,128]{3,2,1,0:T(8,128)S(1)}, f32[8,5,8,128]{3,2,1,0:T(8,128)S(1)}, f32[4,5,2,8,128]{4,3,2,1,0:T(8,128)S(1)}, f32[4,5,2,8,128]{4,3,2,1,...) custom-call(s32[164]{0:T(256)S(1)} %get-tuple-element.28.table, ...), custom_call_target="tpu_custom_call" | custom-call | tf_op jit(solution)/shard_map/pallas_call | solution.py:672
  46.3 0.1 collective-permute-start.6
  46.4 2.5 %collective-permute-start.7 = (f32[2,5,2,8,128]{4,3,2,1,0:T(8,128)S(1)}, f32[2,5,2,8,128]{4,3,2,1,0:T(8,128)S(1)}, u32[]{:S(2)}, u32[]{:S(2)}) collective-permute-start(f32[2,5,2,8,128]{4,3,2,1,0:T(8,128)S(1)} %get-tuple-element.51), channel_id=1, source_target_pairs={{0,1},{1,0},{2,3},{3,2},{4,5},{5,4},{6,7},{7,6},{14,15},{15,14},{1... | collective-permute-start | bytes 245768 | tf_op jit(solution)/shard_map/ppermute | solution.py:686
  48.9 0.0 collective-permute-start.4
  48.9 1.4 %collective-permute-start.5 = (f32[80,128]{1,0:T(8,128)S(1)}, f32[80,128]{1,0:T(8,128)S(1)}, u32[]{:S(2)}, u32[]{:S(2)}) collective-permute-start(f32[80,128]{1,0:T(8,128)S(1)} %get-tuple-element.49), channel_id=1, source_target_pairs={{0,8},{1,9},{2,0},{3,1},{4,2},{5,3},{6,4},{7,5},{14,6},{15,7},{12,... | collective-permute-start | bytes 122888 | tf_op jit(solution)/shard_map/ppermute | solution.py:686
  50.4 1.2 %shard_map.81.corrected = f32[4,5,2,8,128]{4,3,2,1,0:T(8,128)S(1)} custom-call(s32[164]{0:T(256)S(1)} %get-tuple-element.28.table, f32[3,5]{1,0:T(4,128)S(1)} %copy-done.2, f32[8,5,8,128]{3,2,1,0:T(8,128)S(1)} %get-tuple-element.38.fine0.old0, f32[8,5,8,128]{3,2,1,0:T(8,128)S(1)} %get-tuple-element.39.fine1.old1, ...), custom_call_target="tpu_custom_call" | custom-call | tf_op jit(solution)/shard_map/pallas_call | solution.py:672
  51.5 0.2 collective-permute-done.4.below
  51.7 0.3 collective-permute-done.5.above
  52.1 0.0 collective-permute-done.6.outer
  52.1 0.0 collective-permute-done.7.inner
  52.1 2.7 %shard_map.82 = f32[16,128,128]{2,1,0:T(8,128)S(1)} custom-call(s32[164]{0:T(256)S(1)} %get-tuple-element.28.table, f32[3,5]{1,0:T(4,128)S(1)} %copy-done.2, f32[5,5]{1,0:T(8,128)S(1)} %copy-done.1, f32[8,5,8,128]{3,2,1,0:T(8,128)S(1)} %get-tuple-element.38.fine0.old0, f32[8,5,8,128]{3,2,1,0:T(8,128)S(1)} %get-tuple-element.39.fine1.old1, ...), custom_call_target="tpu_custom_call" | custom-call | tf_op jit(solution)/shard_map/pallas_call | solution.py:672
  54.8 20.0 %all_to_all.11.received = f32[16,128,128]{2,1,0:T(8,128)S(1)} all-to-all(f32[16,128,128]{2,1,0:T(8,128)S(1)} %shard_map.82), channel_id=1, replica_groups=mesh['gx'=16,'gy'=16] {'gy'}, dimensions={0} | all-to-all | bytes 2097152 | tf_op jit(solution)/shard_map/all_to_all | solution.py:695
  74.8 2.2 %shard_map.83 = (f32[5,8,8,128]{3,2,1,0:T(8,128)}, f32[2,5,16,16,128]{4,3,2,1,0:T(8,128)}) custom-call(s32[164]{0:T(256)S(1)} %get-tuple-element.28.table, f32[16,128,128]{2,1,0:T(8,128)S(1)} %all_to_all.11.received, f32[2,5,16,16,128]{4,3,2,1,0:T(8,128)S(1)} %shard_map.79.interior), custom_call_target="tpu_custom_call" | custom-call | tf_op jit(solution)/shard_map/pallas_call | solution.py:672
Async XLA Ops:
  30.6 10.2 %copy-start = (f32[2,5,16,16,128]{4,3,2,1,0:T(8,128)S(1)}, f32[2,5,16,16,128]{4,3,2,1,0:T(8,128)}, u32[]{:S(2)}) copy-start(f32[2,5,16,16,128]{4,3,2,1,0:T(8,128)} %fine) | copy-start | bytes 3932164
  30.6 10.2 %copy-start.1 = (f32[5,5]{1,0:T(8,128)S(1)}, f32[5,5]{1,0:T(8,128)}, u32[]{:S(2)}) copy-start(f32[5,5]{1,0:T(8,128)} %reaction.5) | copy-start | bytes 304
  30.6 10.2 %copy-start.2 = (f32[3,5]{1,0:T(4,128)S(1)}, f32[3,5]{1,0:T(4,128)}, u32[]{:S(2)}) copy-start(f32[3,5]{1,0:T(4,128)} %courant.7) | copy-start | bytes 184
  31.6 12.5 %collective-permute-start.2 = (f32[2,5,2,8,128]{4,3,2,1,0:T(8,128)S(1)}, f32[2,5,2,8,128]{4,3,2,1,0:T(8,128)S(1)}, u32[]{:S(2)}, u32[]{:S(2)}) collective-permute-start(f32[2,5,2,8,128]{4,3,2,1,0:T(8,128)S(1)} %get-tuple-element.36), channel_id=1, source_target_pairs={{0,249},{1,24},{2,251},{3,26},{4,253},{5,28},{6,255},{7,30},{14,24... | collective-permute-start | bytes 245768 | tf_op jit(solution)/shard_map/ppermute | solution.py:686
  34.2 9.8 %collective-permute-start.3 = (f32[2,5,2,8,128]{4,3,2,1,0:T(8,128)S(1)}, f32[2,5,2,8,128]{4,3,2,1,0:T(8,128)S(1)}, u32[]{:S(2)}, u32[]{:S(2)}) collective-permute-start(f32[2,5,2,8,128]{4,3,2,1,0:T(8,128)S(1)} %get-tuple-element.37), channel_id=1, source_target_pairs={{0,1},{1,0},{2,3},{3,2},{4,5},{5,4},{6,7},{7,6},{14,15},{15,14},{1... | collective-permute-start | bytes 245768 | tf_op jit(solution)/shard_map/ppermute | solution.py:686
  39.4 4.6 %collective-permute-start = (f32[80,128]{1,0:T(8,128)S(1)}, f32[80,128]{1,0:T(8,128)S(1)}, u32[]{:S(2)}, u32[]{:S(2)}) collective-permute-start(f32[80,128]{1,0:T(8,128)S(1)} %get-tuple-element.34), channel_id=1, source_target_pairs={{0,2},{1,3},{2,4},{3,5},{4,6},{5,7},{6,14},{7,15},{14,12},{15,13},... | collective-permute-start | bytes 122888 | tf_op jit(solution)/shard_map/ppermute | solution.py:686
  39.6 4.5 %collective-permute-start.1 = (f32[80,128]{1,0:T(8,128)S(1)}, f32[80,128]{1,0:T(8,128)S(1)}, u32[]{:S(2)}, u32[]{:S(2)}) collective-permute-start(f32[80,128]{1,0:T(8,128)S(1)} %get-tuple-element.35), channel_id=1, source_target_pairs={{0,8},{1,9},{2,0},{3,1},{4,2},{5,3},{6,4},{7,5},{14,6},{15,7},{12,... | collective-permute-start | bytes 122888 | tf_op jit(solution)/shard_map/ppermute | solution.py:686
  46.3 5.8 %collective-permute-start.6 = (f32[2,5,2,8,128]{4,3,2,1,0:T(8,128)S(1)}, f32[2,5,2,8,128]{4,3,2,1,0:T(8,128)S(1)}, u32[]{:S(2)}, u32[]{:S(2)}) collective-permute-start(f32[2,5,2,8,128]{4,3,2,1,0:T(8,128)S(1)} %get-tuple-element.50), channel_id=1, source_target_pairs={{0,249},{1,24},{2,251},{3,26},{4,253},{5,28},{6,255},{7,30},{14,24... | collective-permute-start | bytes 245768 | tf_op jit(solution)/shard_map/ppermute | solution.py:686
  46.4 5.7 %collective-permute-start.7 = (f32[2,5,2,8,128]{4,3,2,1,0:T(8,128)S(1)}, f32[2,5,2,8,128]{4,3,2,1,0:T(8,128)S(1)}, u32[]{:S(2)}, u32[]{:S(2)}) collective-permute-start(f32[2,5,2,8,128]{4,3,2,1,0:T(8,128)S(1)} %get-tuple-element.51), channel_id=1, source_target_pairs={{0,1},{1,0},{2,3},{3,2},{4,5},{5,4},{6,7},{7,6},{14,15},{15,14},{1... | collective-permute-start | bytes 245768 | tf_op jit(solution)/shard_map/ppermute | solution.py:686
  48.9 2.9 %collective-permute-start.4 = (f32[80,128]{1,0:T(8,128)S(1)}, f32[80,128]{1,0:T(8,128)S(1)}, u32[]{:S(2)}, u32[]{:S(2)}) collective-permute-start(f32[80,128]{1,0:T(8,128)S(1)} %get-tuple-element.48), channel_id=1, source_target_pairs={{0,2},{1,3},{2,4},{3,5},{4,6},{5,7},{6,14},{7,15},{14,12},{15,13},... | collective-permute-start | bytes 122888 | tf_op jit(solution)/shard_map/ppermute | solution.py:686
  48.9 3.1 %collective-permute-start.5 = (f32[80,128]{1,0:T(8,128)S(1)}, f32[80,128]{1,0:T(8,128)S(1)}, u32[]{:S(2)}, u32[]{:S(2)}) collective-permute-start(f32[80,128]{1,0:T(8,128)S(1)} %get-tuple-element.49), channel_id=1, source_target_pairs={{0,8},{1,9},{2,0},{3,1},{4,2},{5,3},{6,4},{7,5},{14,6},{15,7},{12,... | collective-permute-start | bytes 122888 | tf_op jit(solution)/shard_map/ppermute | solution.py:686
where the time goes:
time: 77.2 us; the launch traced here: 77 us
  blocking collectives  47.1 us (61%)
  Pallas kernels  15.3 us (20%)
  starting transfers between devices  13.3 us (17%)
    all_to_all x2, blocking collectives, spread(): return lax.all_to_all(pieces, 'gy', 0, 0, tiled=True)  47.1 us
    pallas_call x7, Pallas kernels, call(): pl.pallas_call(kernel, out_shape=out_shape, in_specs=[SMEM] * smem + [in_...  15.3 us
    ppermute x8, starting transfers between devices, exchange(): lax.ppermute(value, axes, [(device(*d), device(*target(*d))) for d in all...  13.3 us
  transfers between devices with their start and end apart: 8, of which 2 were waited for; matrix products, arithmetic and copies ran while one was open for 0% of the time, Pallas kernels for 6%

commit v1 on v0

--- a/solution.py
+++ b/solution.py
@@ -109,10 +109,13 @@
     )
     for load in (*integers, *loads):
         load.start()
-    for load in (*integers, *loads):
+    for load in (*integers, *loads[:SPECIES]):
         load.wait()
     fill_table(corners, sources, table, listed, ranks)
     for n, (k, s) in enumerate(blocks):
+        if n == SPECIES:
+            for load in loads[SPECIES:]:
+                load.wait()
         turned = fine[k, s].reshape(256, 128).T
         at = (k * SPECIES + s) * 16
         for m in range(CHUNKS):
@@ -215,7 +218,7 @@
                     store(s, x, j, moved(values[j], upwind, size, weights, s))
             return carry
 
-        lax.fori_loop(first, last, plane, 0, unroll=2)
+        lax.fori_loop(first, last, plane, 0, unroll=True)
 
     for k in range(2):
 

time: 77.2 us -> 76.6 us (level)
  Pallas kernels: 15.3 us -> 13.8 us
  starting transfers between devices: 13.3 us -> 14.5 us
    pallas_call x7, Pallas kernels: 15.3 us -> 13.8 us  [call(): pl.pallas_call(kernel, out_shape=out_shape, in_specs=[SMEM] * smem + [in_...]
    ppermute x8, starting transfers between devices: 13.3 us -> 14.5 us  [exchange(): lax.ppermute(value, axes, [(device(*d), device(*target(*d))) for d in all...]
  transfers between devices with their start and end apart: 8 -> 8, of which waited for: 2 -> 1; matrix products, arithmetic and copies ran while one was open for 0% -> 0% of each run, Pallas kernels for 6% -> 4%
where the time goes in v1:
time: 76.6 us; the launch traced here: 76.4 us
  blocking collectives  46.7 us (61%)
  starting transfers between devices  14.5 us (19%)
  Pallas kernels  13.8 us (18%)
    all_to_all x2, blocking collectives, spread(): return lax.all_to_all(pieces, 'gy', 0, 0, tiled=True)  46.7 us
    ppermute x8, starting transfers between devices, exchange(): lax.ppermute(value, axes, [(device(*d), device(*target(*d))) for d in all...  14.5 us
    pallas_call x7, Pallas kernels, call(): pl.pallas_call(kernel, out_shape=out_shape, in_specs=[SMEM] * smem + [in_...  13.8 us
  transfers between devices with their start and end apart: 8, of which 1 were waited for; matrix products, arithmetic and copies ran while one was open for 0% of the time, Pallas kernels for 4%

profile of v1, /device:TPU:1, one launch (start us, length us, event | category | flops | bytes accessed | tf_op | source)
XLA Modules:
  0.0 76.4 jit_solution(16155378097408122003)
XLA Ops:
  0.6 2.7 %shard_map.77 = (f32[16,184,128]{2,1,0:T(8,128)S(1)}, s32[164]{0:T(256)S(1)}) custom-call(s32[3,512]{1,0:T(4,128)} %bitcast.3, s32[6,512]{1,0:T(8,128)} %bitcast.2, f32[5,8,8,128]{3,2,1,0:T(8,128)} %coarse_in.1, f32[2,5,16,16,128]{4,3,2,1,0:T(8,128)} %fine), custom_call_target="tpu_custom_call" | custom-call | tf_op jit(solution)/shard_map/pallas_call | solution.py:675
  3.3 27.0 %all_to_all.10.received = f32[16,184,128]{2,1,0:T(8,128)S(1)} all-to-all(f32[16,184,128]{2,1,0:T(8,128)S(1)} %get-tuple-element.29), channel_id=1, replica_groups=mesh['gx'=16,'gy'=16] {'gy'}, dimensions={0} | all-to-all | bytes 3014656 | tf_op jit(solution)/shard_map/all_to_all | solution.py:698
  30.3 0.0 copy-start
  30.3 0.0 copy-start.1
  30.3 0.0 copy-start.2
  30.3 0.9 %shard_map.78 = (f32[8,5,8,128]{3,2,1,0:T(8,128)S(1)}, f32[8,5,8,128]{3,2,1,0:T(8,128)S(1)}, f32[4,5,2,8,128]{4,3,2,1,0:T(8,128)S(1)}, f32[80,128]{1,0:T(8,128)S...) custom-call(s32[164]{0:T(256)S(1)} %get-tuple-element.28.table, ...), custom_call_target="tpu_custom_call" | custom-call | tf_op jit(solution)/shard_map/pallas_call | solution.py:675
  31.3 2.7 %collective-permute-start.2 = (f32[2,5,2,8,128]{4,3,2,1,0:T(8,128)S(1)}, f32[2,5,2,8,128]{4,3,2,1,0:T(8,128)S(1)}, u32[]{:S(2)}, u32[]{:S(2)}) collective-permute-start(f32[2,5,2,8,128]{4,3,2,1,0:T(8,128)S(1)} %get-tuple-element.36), channel_id=1, source_target_pairs={{0,249},{1,24},{2,251},{3,26},{4,253},{5,28},{6,255},{7,30},{14,24... | collective-permute-start | bytes 245768 | tf_op jit(solution)/shard_map/ppermute | solution.py:689
  33.9 5.2 %collective-permute-start.3 = (f32[2,5,2,8,128]{4,3,2,1,0:T(8,128)S(1)}, f32[2,5,2,8,128]{4,3,2,1,0:T(8,128)S(1)}, u32[]{:S(2)}, u32[]{:S(2)}) collective-permute-start(f32[2,5,2,8,128]{4,3,2,1,0:T(8,128)S(1)} %get-tuple-element.37), channel_id=1, source_target_pairs={{0,1},{1,0},{2,3},{3,2},{4,5},{5,4},{6,7},{7,6},{14,15},{15,14},{1... | collective-permute-start | bytes 245768 | tf_op jit(solution)/shard_map/ppermute | solution.py:689
  39.1 0.2 collective-permute-start
  39.3 1.3 %collective-permute-start.1 = (f32[80,128]{1,0:T(8,128)S(1)}, f32[80,128]{1,0:T(8,128)S(1)}, u32[]{:S(2)}, u32[]{:S(2)}) collective-permute-start(f32[80,128]{1,0:T(8,128)S(1)} %get-tuple-element.35), channel_id=1, source_target_pairs={{0,8},{1,9},{2,0},{3,1},{4,2},{5,3},{6,4},{7,5},{14,6},{15,7},{12,... | collective-permute-start | bytes 122888 | tf_op jit(solution)/shard_map/ppermute | solution.py:689
  40.6 0.0 copy-done
  40.6 0.0 copy-done.1
  40.6 0.0 copy-done.2
  40.6 2.0 %shard_map.79.interior = f32[2,5,16,16,128]{4,3,2,1,0:T(8,128)S(1)} custom-call(f32[3,5]{1,0:T(4,128)S(1)} %copy-done.2, f32[5,5]{1,0:T(8,128)S(1)} %copy-done.1, f32[2,5,16,16,128]{4,3,2,1,0:T(8,128)S(1)} %copy-done), custom_call_target="tpu_custom_call" | custom-call | tf_op jit(solution)/shard_map/pallas_call | solution.py:675
  42.6 0.0 collective-permute-done.below.old_below
  42.6 0.0 collective-permute-done.1.above.old_above
  42.6 0.0 collective-permute-done.2.outer.old_outer
  42.6 0.0 collective-permute-done.3.inner.old_inner
  42.6 2.2 %shard_map.80 = (f32[8,5,8,128]{3,2,1,0:T(8,128)S(1)}, f32[8,5,8,128]{3,2,1,0:T(8,128)S(1)}, f32[4,5,2,8,128]{4,3,2,1,0:T(8,128)S(1)}, f32[4,5,2,8,128]{4,3,2,1,...) custom-call(s32[164]{0:T(256)S(1)} %get-tuple-element.28.table, ...), custom_call_target="tpu_custom_call" | custom-call | tf_op jit(solution)/shard_map/pallas_call | solution.py:675
  44.8 0.1 collective-permute-start.6
  44.9 3.6 %collective-permute-start.7 = (f32[2,5,2,8,128]{4,3,2,1,0:T(8,128)S(1)}, f32[2,5,2,8,128]{4,3,2,1,0:T(8,128)S(1)}, u32[]{:S(2)}, u32[]{:S(2)}) collective-permute-start(f32[2,5,2,8,128]{4,3,2,1,0:T(8,128)S(1)} %get-tuple-element.51), channel_id=1, source_target_pairs={{0,1},{1,0},{2,3},{3,2},{4,5},{5,4},{6,7},{7,6},{14,15},{15,14},{1... | collective-permute-start | bytes 245768 | tf_op jit(solution)/shard_map/ppermute | solution.py:689
  48.6 0.0 collective-permute-start.4
  48.6 1.4 %collective-permute-start.5 = (f32[80,128]{1,0:T(8,128)S(1)}, f32[80,128]{1,0:T(8,128)S(1)}, u32[]{:S(2)}, u32[]{:S(2)}) collective-permute-start(f32[80,128]{1,0:T(8,128)S(1)} %get-tuple-element.49), channel_id=1, source_target_pairs={{0,8},{1,9},{2,0},{3,1},{4,2},{5,3},{6,4},{7,5},{14,6},{15,7},{12,... | collective-permute-start | bytes 122888 | tf_op jit(solution)/shard_map/ppermute | solution.py:689
  50.0 1.2 %shard_map.81.corrected = f32[4,5,2,8,128]{4,3,2,1,0:T(8,128)S(1)} custom-call(s32[164]{0:T(256)S(1)} %get-tuple-element.28.table, f32[3,5]{1,0:T(4,128)S(1)} %copy-done.2, f32[8,5,8,128]{3,2,1,0:T(8,128)S(1)} %get-tuple-element.38.fine0.old0, f32[8,5,8,128]{3,2,1,0:T(8,128)S(1)} %get-tuple-element.39.fine1.old1, ...), custom_call_target="tpu_custom_call" | custom-call | tf_op jit(solution)/shard_map/pallas_call | solution.py:675
  51.2 0.5 collective-permute-done.4.below
  51.7 0.0 collective-permute-done.5.above
  51.8 0.0 collective-permute-done.6.outer
  51.8 0.0 collective-permute-done.7.inner
  51.8 2.7 %shard_map.82 = f32[16,128,128]{2,1,0:T(8,128)S(1)} custom-call(s32[164]{0:T(256)S(1)} %get-tuple-element.28.table, f32[3,5]{1,0:T(4,128)S(1)} %copy-done.2, f32[5,5]{1,0:T(8,128)S(1)} %copy-done.1, f32[8,5,8,128]{3,2,1,0:T(8,128)S(1)} %get-tuple-element.38.fine0.old0, f32[8,5,8,128]{3,2,1,0:T(8,128)S(1)} %get-tuple-element.39.fine1.old1, ...), custom_call_target="tpu_custom_call" | custom-call | tf_op jit(solution)/shard_map/pallas_call | solution.py:675
  54.5 19.7 %all_to_all.11.received = f32[16,128,128]{2,1,0:T(8,128)S(1)} all-to-all(f32[16,128,128]{2,1,0:T(8,128)S(1)} %shard_map.82), channel_id=1, replica_groups=mesh['gx'=16,'gy'=16] {'gy'}, dimensions={0} | all-to-all | bytes 2097152 | tf_op jit(solution)/shard_map/all_to_all | solution.py:698
  74.2 2.2 %shard_map.83 = (f32[5,8,8,128]{3,2,1,0:T(8,128)}, f32[2,5,16,16,128]{4,3,2,1,0:T(8,128)}) custom-call(s32[164]{0:T(256)S(1)} %get-tuple-element.28.table, f32[16,128,128]{2,1,0:T(8,128)S(1)} %all_to_all.11.received, f32[2,5,16,16,128]{4,3,2,1,0:T(8,128)S(1)} %shard_map.79.interior), custom_call_target="tpu_custom_call" | custom-call | tf_op jit(solution)/shard_map/pallas_call | solution.py:675
Async XLA Ops:
  30.3 10.2 %copy-start = (f32[2,5,16,16,128]{4,3,2,1,0:T(8,128)S(1)}, f32[2,5,16,16,128]{4,3,2,1,0:T(8,128)}, u32[]{:S(2)}) copy-start(f32[2,5,16,16,128]{4,3,2,1,0:T(8,128)} %fine) | copy-start | bytes 3932164
  30.3 10.2 %copy-start.1 = (f32[5,5]{1,0:T(8,128)S(1)}, f32[5,5]{1,0:T(8,128)}, u32[]{:S(2)}) copy-start(f32[5,5]{1,0:T(8,128)} %reaction.5) | copy-start | bytes 304
  30.3 10.2 %copy-start.2 = (f32[3,5]{1,0:T(4,128)S(1)}, f32[3,5]{1,0:T(4,128)}, u32[]{:S(2)}) copy-start(f32[3,5]{1,0:T(4,128)} %courant.7) | copy-start | bytes 184
  31.3 11.3 %collective-permute-start.2 = (f32[2,5,2,8,128]{4,3,2,1,0:T(8,128)S(1)}, f32[2,5,2,8,128]{4,3,2,1,0:T(8,128)S(1)}, u32[]{:S(2)}, u32[]{:S(2)}) collective-permute-start(f32[2,5,2,8,128]{4,3,2,1,0:T(8,128)S(1)} %get-tuple-element.36), channel_id=1, source_target_pairs={{0,249},{1,24},{2,251},{3,26},{4,253},{5,28},{6,255},{7,30},{14,24... | collective-permute-start | bytes 245768 | tf_op jit(solution)/shard_map/ppermute | solution.py:689
  33.9 8.7 %collective-permute-start.3 = (f32[2,5,2,8,128]{4,3,2,1,0:T(8,128)S(1)}, f32[2,5,2,8,128]{4,3,2,1,0:T(8,128)S(1)}, u32[]{:S(2)}, u32[]{:S(2)}) collective-permute-start(f32[2,5,2,8,128]{4,3,2,1,0:T(8,128)S(1)} %get-tuple-element.37), channel_id=1, source_target_pairs={{0,1},{1,0},{2,3},{3,2},{4,5},{5,4},{6,7},{7,6},{14,15},{15,14},{1... | collective-permute-start | bytes 245768 | tf_op jit(solution)/shard_map/ppermute | solution.py:689
  39.1 3.5 %collective-permute-start = (f32[80,128]{1,0:T(8,128)S(1)}, f32[80,128]{1,0:T(8,128)S(1)}, u32[]{:S(2)}, u32[]{:S(2)}) collective-permute-start(f32[80,128]{1,0:T(8,128)S(1)} %get-tuple-element.34), channel_id=1, source_target_pairs={{0,2},{1,3},{2,4},{3,5},{4,6},{5,7},{6,14},{7,15},{14,12},{15,13},... | collective-permute-start | bytes 122888 | tf_op jit(solution)/shard_map/ppermute | solution.py:689
  39.3 3.3 %collective-permute-start.1 = (f32[80,128]{1,0:T(8,128)S(1)}, f32[80,128]{1,0:T(8,128)S(1)}, u32[]{:S(2)}, u32[]{:S(2)}) collective-permute-start(f32[80,128]{1,0:T(8,128)S(1)} %get-tuple-element.35), channel_id=1, source_target_pairs={{0,8},{1,9},{2,0},{3,1},{4,2},{5,3},{6,4},{7,5},{14,6},{15,7},{12,... | collective-permute-start | bytes 122888 | tf_op jit(solution)/shard_map/ppermute | solution.py:689
  44.8 6.9 %collective-permute-start.6 = (f32[2,5,2,8,128]{4,3,2,1,0:T(8,128)S(1)}, f32[2,5,2,8,128]{4,3,2,1,0:T(8,128)S(1)}, u32[]{:S(2)}, u32[]{:S(2)}) collective-permute-start(f32[2,5,2,8,128]{4,3,2,1,0:T(8,128)S(1)} %get-tuple-element.50), channel_id=1, source_target_pairs={{0,249},{1,24},{2,251},{3,26},{4,253},{5,28},{6,255},{7,30},{14,24... | collective-permute-start | bytes 245768 | tf_op jit(solution)/shard_map/ppermute | solution.py:689
  44.9 6.8 %collective-permute-start.7 = (f32[2,5,2,8,128]{4,3,2,1,0:T(8,128)S(1)}, f32[2,5,2,8,128]{4,3,2,1,0:T(8,128)S(1)}, u32[]{:S(2)}, u32[]{:S(2)}) collective-permute-start(f32[2,5,2,8,128]{4,3,2,1,0:T(8,128)S(1)} %get-tuple-element.51), channel_id=1, source_target_pairs={{0,1},{1,0},{2,3},{3,2},{4,5},{5,4},{6,7},{7,6},{14,15},{15,14},{1... | collective-permute-start | bytes 245768 | tf_op jit(solution)/shard_map/ppermute | solution.py:689
  48.6 3.1 %collective-permute-start.4 = (f32[80,128]{1,0:T(8,128)S(1)}, f32[80,128]{1,0:T(8,128)S(1)}, u32[]{:S(2)}, u32[]{:S(2)}) collective-permute-start(f32[80,128]{1,0:T(8,128)S(1)} %get-tuple-element.48), channel_id=1, source_target_pairs={{0,2},{1,3},{2,4},{3,5},{4,6},{5,7},{6,14},{7,15},{14,12},{15,13},... | collective-permute-start | bytes 122888 | tf_op jit(solution)/shard_map/ppermute | solution.py:689
  48.6 3.1 %collective-permute-start.5 = (f32[80,128]{1,0:T(8,128)S(1)}, f32[80,128]{1,0:T(8,128)S(1)}, u32[]{:S(2)}, u32[]{:S(2)}) collective-permute-start(f32[80,128]{1,0:T(8,128)S(1)} %get-tuple-element.49), channel_id=1, source_target_pairs={{0,8},{1,9},{2,0},{3,1},{4,2},{5,3},{6,4},{7,5},{14,6},{15,7},{12,... | collective-permute-start | bytes 122888 | tf_op jit(solution)/shard_map/ppermute | solution.py:689

commit v2 on v1

--- a/solution.py
+++ b/solution.py
@@ -26,7 +26,7 @@
 TABLE = OWN + 4
 SHELL_ROWS = 80
 PLANE_ROWS = 104
-BACK_ROWS = 128
+BACK_ROWS = 120
 
 VMEM = pl.BlockSpec(memory_space=pltpu.VMEM)
 SMEM = pl.BlockSpec(memory_space=pltpu.SMEM)
@@ -148,18 +148,25 @@
     live = [table[OWN + 2 * k] > 0 for k in range(2)]
     high = [table[OWN + 2 * k + 1] > 0 for k in range(2)]
     in_plane = [jnp.where(high[k], lanes, 127 - lanes) < 2 for k in range(2)]
+    turned = lax.rem(column, 4)
     for part in range(2):
-        parts = []
+        parts, last = [], []
         for k in range(2):
             source = jnp.where(high[k], device_of(0, part, row), device_of(CHUNKS - 1, part, row))
-            parts.append(received[source, PLANE_ROWS + 10 * k : PLANE_ROWS + 10 * k + 10, :])
-        planes[part] = jnp.concatenate([*parts, jnp.zeros((108, 128), F32)]).T
+            parts.append(received[source, PLANE_ROWS + 8 * k : PLANE_ROWS + 8 * k + 8, :])
+            tile = received[source, PLANE_ROWS - 8 : PLANE_ROWS, :]
+            low = pltpu.roll(tile, lax.rem(192 - 32 * turned, 128), 1)
+            rest = pltpu.roll(turn(tile, -2, 0), lax.rem(128 - 32 * turned, 128), 1)
+            last.append(jnp.where(lanes < 64, low, rest))
+        parts.append(jnp.where(rows < 4, last[0], last[1]))
+        planes[part] = jnp.concatenate([*parts, jnp.zeros((104, 128), F32)]).T
     for s in range(SPECIES):
         for part in range(2):
             pieces = [received[device_of(m, part, row), 16 * s : 16 * s + 16, :] for m in range(CHUNKS)]
             shells[part] = jnp.concatenate(pieces).T
         for k in range(2):
-            shift = lax.rem(jnp.where(high[k], 128, 254) - (10 * k + 2 * s), 128)
+            first = 8 * k + 2 * s if s < SPECIES - 1 else 16 + 4 * k
+            shift = lax.rem(jnp.where(high[k], 128, 254) - first, 128)
             for x in range(16):
                 part, at_x = x // 8, x % 8
                 depth = at_x if part == 0 else 7 - at_x
@@ -588,8 +595,9 @@
                 at = (2 * s + r) * 8
                 packed = take(result[i, s], shell_index, 1)
                 out[t // 2, at : at + 8, :] = jnp.where(mine, packed, out[t // 2, at : at + 8, :])
-            plane = jnp.where(m == 0, result0[i, s, 0:2, :], result1[i, s, 6:8, :])
-            out[t // 2, pl.ds(PLANE_ROWS + 10 * k + 2 * s, 2), :] = plane
+            if s < SPECIES - 1:
+                plane = jnp.where(m == 0, result0[i, s, 0:2, :], result1[i, s, 6:8, :])
+                out[t // 2, pl.ds(PLANE_ROWS + 8 * k + 2 * s, 2), :] = plane
         return carry
 
     lax.fori_loop(0, BOXES, pack_box, 0, unroll=4)
@@ -667,6 +675,20 @@
                 for k in range(1, len(tiles)):
                     tile = jnp.where(group == (o + k) % 4, tiles[k], tile)
                 out[4 * q + o, at : at + 8, :] = tile
+
+    def pack_last(i, carry):
+        t = table[STRIDE * i + SLOT]
+        k, o = lax.rem(t, 2), lax.rem(t // 2, 4)
+        plane = jnp.where(m == 0, result0[i, SPECIES - 1], turn(result1[i, SPECIES - 1], 2, 0))
+        low = pltpu.roll(plane, lax.rem(32 * o + 64, 128), 1)
+        high = pltpu.roll(turn(plane, 2, 0), 32 * o, 1)
+        tile = jnp.where(rows < 2, low, high)
+        tile = jnp.where(k > 0, turn(tile, 4, 0), tile)
+        free = (rows // 4 == k) & (lax.rem(group + 4 - o, 4) >= 2)
+        out[t // 2, PLANE_ROWS - 8 : PLANE_ROWS, :] = jnp.where(free, tile, out[t // 2, PLANE_ROWS - 8 : PLANE_ROWS, :])
+        return carry
+
+    lax.fori_loop(0, BOXES, pack_last, 0, unroll=8)
 
 
 def call(kernel, out_shape, operands, smem, scratch=(), in_spec=VMEM, out_spec=VMEM):

time: 76.6 us -> 76 us (level)
  no operation moved by 1% of the time
where the time goes in v2:
time: 76 us; the launch traced here: 75.8 us
  blocking collectives  46 us (61%)
  starting transfers between devices  14.5 us (19%)
  Pallas kernels  14 us (18%)
    all_to_all x2, blocking collectives, spread(): return lax.all_to_all(pieces, 'gy', 0, 0, tiled=True)  46 us
    ppermute x8, starting transfers between devices, exchange(): lax.ppermute(value, axes, [(device(*d), device(*target(*d))) for d in all...  14.5 us
    pallas_call x7, Pallas kernels, call(): pl.pallas_call(kernel, out_shape=out_shape, in_specs=[SMEM] * smem + [in_...  14 us
  transfers between devices with their start and end apart: 8, of which 1 were waited for; matrix products, arithmetic and copies ran while one was open for 0% of the time, Pallas kernels for 4%

profile of v2, /device:TPU:1, one launch (start us, length us, event | category | flops | bytes accessed | tf_op | source)
XLA Modules:
  0.0 75.8 jit_solution(10265080385382065509)
XLA Ops:
  0.6 2.7 %shard_map.77 = (f32[16,184,128]{2,1,0:T(8,128)S(1)}, s32[164]{0:T(256)S(1)}) custom-call(s32[3,512]{1,0:T(4,128)} %bitcast.3, s32[6,512]{1,0:T(8,128)} %bitcast.2, f32[5,8,8,128]{3,2,1,0:T(8,128)} %coarse_in.1, f32[2,5,16,16,128]{4,3,2,1,0:T(8,128)} %fine), custom_call_target="tpu_custom_call" | custom-call | tf_op jit(solution)/shard_map/pallas_call | solution.py:697
  3.3 27.0 %all_to_all.10.received = f32[16,184,128]{2,1,0:T(8,128)S(1)} all-to-all(f32[16,184,128]{2,1,0:T(8,128)S(1)} %get-tuple-element.29), channel_id=1, replica_groups=mesh['gx'=16,'gy'=16] {'gy'}, dimensions={0} | all-to-all | bytes 3014656 | tf_op jit(solution)/shard_map/all_to_all | solution.py:720
  30.3 0.0 copy-start
  30.3 0.0 copy-start.1
  30.3 0.0 copy-start.2
  30.3 0.9 %shard_map.78 = (f32[8,5,8,128]{3,2,1,0:T(8,128)S(1)}, f32[8,5,8,128]{3,2,1,0:T(8,128)S(1)}, f32[4,5,2,8,128]{4,3,2,1,0:T(8,128)S(1)}, f32[80,128]{1,0:T(8,128)S...) custom-call(s32[164]{0:T(256)S(1)} %get-tuple-element.28.table, ...), custom_call_target="tpu_custom_call" | custom-call | tf_op jit(solution)/shard_map/pallas_call | solution.py:697
  31.3 2.7 %collective-permute-start.2 = (f32[2,5,2,8,128]{4,3,2,1,0:T(8,128)S(1)}, f32[2,5,2,8,128]{4,3,2,1,0:T(8,128)S(1)}, u32[]{:S(2)}, u32[]{:S(2)}) collective-permute-start(f32[2,5,2,8,128]{4,3,2,1,0:T(8,128)S(1)} %get-tuple-element.36), channel_id=1, source_target_pairs={{0,249},{1,24},{2,251},{3,26},{4,253},{5,28},{6,255},{7,30},{14,24... | collective-permute-start | bytes 245768 | tf_op jit(solution)/shard_map/ppermute | solution.py:711
  33.9 5.1 %collective-permute-start.3 = (f32[2,5,2,8,128]{4,3,2,1,0:T(8,128)S(1)}, f32[2,5,2,8,128]{4,3,2,1,0:T(8,128)S(1)}, u32[]{:S(2)}, u32[]{:S(2)}) collective-permute-start(f32[2,5,2,8,128]{4,3,2,1,0:T(8,128)S(1)} %get-tuple-element.37), channel_id=1, source_target_pairs={{0,1},{1,0},{2,3},{3,2},{4,5},{5,4},{6,7},{7,6},{14,15},{15,14},{1... | collective-permute-start | bytes 245768 | tf_op jit(solution)/shard_map/ppermute | solution.py:711
  39.1 0.2 collective-permute-start
  39.3 1.3 %collective-permute-start.1 = (f32[80,128]{1,0:T(8,128)S(1)}, f32[80,128]{1,0:T(8,128)S(1)}, u32[]{:S(2)}, u32[]{:S(2)}) collective-permute-start(f32[80,128]{1,0:T(8,128)S(1)} %get-tuple-element.35), channel_id=1, source_target_pairs={{0,8},{1,9},{2,0},{3,1},{4,2},{5,3},{6,4},{7,5},{14,6},{15,7},{12,... | collective-permute-start | bytes 122888 | tf_op jit(solution)/shard_map/ppermute | solution.py:711
  40.6 0.0 copy-done
  40.6 0.0 copy-done.1
  40.6 0.0 copy-done.2
  40.6 2.0 %shard_map.79.interior = f32[2,5,16,16,128]{4,3,2,1,0:T(8,128)S(1)} custom-call(f32[3,5]{1,0:T(4,128)S(1)} %copy-done.2, f32[5,5]{1,0:T(8,128)S(1)} %copy-done.1, f32[2,5,16,16,128]{4,3,2,1,0:T(8,128)S(1)} %copy-done), custom_call_target="tpu_custom_call" | custom-call | tf_op jit(solution)/shard_map/pallas_call | solution.py:697
  42.6 0.0 collective-permute-done.below.old_below
  42.6 0.0 collective-permute-done.1.above.old_above
  42.6 0.0 collective-permute-done.2.outer.old_outer
  42.6 0.0 collective-permute-done.3.inner.old_inner
  42.6 2.2 %shard_map.80 = (f32[8,5,8,128]{3,2,1,0:T(8,128)S(1)}, f32[8,5,8,128]{3,2,1,0:T(8,128)S(1)}, f32[4,5,2,8,128]{4,3,2,1,0:T(8,128)S(1)}, f32[4,5,2,8,128]{4,3,2,1,...) custom-call(s32[164]{0:T(256)S(1)} %get-tuple-element.28.table, ...), custom_call_target="tpu_custom_call" | custom-call | tf_op jit(solution)/shard_map/pallas_call | solution.py:697
  44.8 0.1 collective-permute-start.6
  44.9 3.7 %collective-permute-start.7 = (f32[2,5,2,8,128]{4,3,2,1,0:T(8,128)S(1)}, f32[2,5,2,8,128]{4,3,2,1,0:T(8,128)S(1)}, u32[]{:S(2)}, u32[]{:S(2)}) collective-permute-start(f32[2,5,2,8,128]{4,3,2,1,0:T(8,128)S(1)} %get-tuple-element.51), channel_id=1, source_target_pairs={{0,1},{1,0},{2,3},{3,2},{4,5},{5,4},{6,7},{7,6},{14,15},{15,14},{1... | collective-permute-start | bytes 245768 | tf_op jit(solution)/shard_map/ppermute | solution.py:711
  48.6 0.0 collective-permute-start.4
  48.6 1.4 %collective-permute-start.5 = (f32[80,128]{1,0:T(8,128)S(1)}, f32[80,128]{1,0:T(8,128)S(1)}, u32[]{:S(2)}, u32[]{:S(2)}) collective-permute-start(f32[80,128]{1,0:T(8,128)S(1)} %get-tuple-element.49), channel_id=1, source_target_pairs={{0,8},{1,9},{2,0},{3,1},{4,2},{5,3},{6,4},{7,5},{14,6},{15,7},{12,... | collective-permute-start | bytes 122888 | tf_op jit(solution)/shard_map/ppermute | solution.py:711
  50.0 1.2 %shard_map.81.corrected = f32[4,5,2,8,128]{4,3,2,1,0:T(8,128)S(1)} custom-call(s32[164]{0:T(256)S(1)} %get-tuple-element.28.table, f32[3,5]{1,0:T(4,128)S(1)} %copy-done.2, f32[8,5,8,128]{3,2,1,0:T(8,128)S(1)} %get-tuple-element.38.fine0.old0, f32[8,5,8,128]{3,2,1,0:T(8,128)S(1)} %get-tuple-element.39.fine1.old1, ...), custom_call_target="tpu_custom_call" | custom-call | tf_op jit(solution)/shard_map/pallas_call | solution.py:697
  51.3 0.5 collective-permute-done.4.below
  51.7 0.0 collective-permute-done.5.above
  51.8 0.0 collective-permute-done.6.outer
  51.8 0.0 collective-permute-done.7.inner
  51.8 2.8 %shard_map.82 = f32[16,120,128]{2,1,0:T(8,128)S(1)} custom-call(s32[164]{0:T(256)S(1)} %get-tuple-element.28.table, f32[3,5]{1,0:T(4,128)S(1)} %copy-done.2, f32[5,5]{1,0:T(8,128)S(1)} %copy-done.1, f32[8,5,8,128]{3,2,1,0:T(8,128)S(1)} %get-tuple-element.38.fine0.old0, f32[8,5,8,128]{3,2,1,0:T(8,128)S(1)} %get-tuple-element.39.fine1.old1, ...), custom_call_target="tpu_custom_call" | custom-call | tf_op jit(solution)/shard_map/pallas_call | solution.py:697
  54.6 19.0 %all_to_all.11.received = f32[16,120,128]{2,1,0:T(8,128)S(1)} all-to-all(f32[16,120,128]{2,1,0:T(8,128)S(1)} %shard_map.82), channel_id=1, replica_groups=mesh['gx'=16,'gy'=16] {'gy'}, dimensions={0} | all-to-all | bytes 1966080 | tf_op jit(solution)/shard_map/all_to_all | solution.py:720
  73.5 2.2 %shard_map.83 = (f32[5,8,8,128]{3,2,1,0:T(8,128)}, f32[2,5,16,16,128]{4,3,2,1,0:T(8,128)}) custom-call(s32[164]{0:T(256)S(1)} %get-tuple-element.28.table, f32[16,120,128]{2,1,0:T(8,128)S(1)} %all_to_all.11.received, f32[2,5,16,16,128]{4,3,2,1,0:T(8,128)S(1)} %shard_map.79.interior), custom_call_target="tpu_custom_call" | custom-call | tf_op jit(solution)/shard_map/pallas_call | solution.py:697
Async XLA Ops:
  30.3 10.2 %copy-start = (f32[2,5,16,16,128]{4,3,2,1,0:T(8,128)S(1)}, f32[2,5,16,16,128]{4,3,2,1,0:T(8,128)}, u32[]{:S(2)}) copy-start(f32[2,5,16,16,128]{4,3,2,1,0:T(8,128)} %fine) | copy-start | bytes 3932164
  30.3 10.2 %copy-start.1 = (f32[5,5]{1,0:T(8,128)S(1)}, f32[5,5]{1,0:T(8,128)}, u32[]{:S(2)}) copy-start(f32[5,5]{1,0:T(8,128)} %reaction.5) | copy-start | bytes 304
  30.3 10.2 %copy-start.2 = (f32[3,5]{1,0:T(4,128)S(1)}, f32[3,5]{1,0:T(4,128)}, u32[]{:S(2)}) copy-start(f32[3,5]{1,0:T(4,128)} %courant.7) | copy-start | bytes 184
  31.3 11.3 %collective-permute-start.2 = (f32[2,5,2,8,128]{4,3,2,1,0:T(8,128)S(1)}, f32[2,5,2,8,128]{4,3,2,1,0:T(8,128)S(1)}, u32[]{:S(2)}, u32[]{:S(2)}) collective-permute-start(f32[2,5,2,8,128]{4,3,2,1,0:T(8,128)S(1)} %get-tuple-element.36), channel_id=1, source_target_pairs={{0,249},{1,24},{2,251},{3,26},{4,253},{5,28},{6,255},{7,30},{14,24... | collective-permute-start | bytes 245768 | tf_op jit(solution)/shard_map/ppermute | solution.py:711
  33.9 8.6 %collective-permute-start.3 = (f32[2,5,2,8,128]{4,3,2,1,0:T(8,128)S(1)}, f32[2,5,2,8,128]{4,3,2,1,0:T(8,128)S(1)}, u32[]{:S(2)}, u32[]{:S(2)}) collective-permute-start(f32[2,5,2,8,128]{4,3,2,1,0:T(8,128)S(1)} %get-tuple-element.37), channel_id=1, source_target_pairs={{0,1},{1,0},{2,3},{3,2},{4,5},{5,4},{6,7},{7,6},{14,15},{15,14},{1... | collective-permute-start | bytes 245768 | tf_op jit(solution)/shard_map/ppermute | solution.py:711
  39.1 3.5 %collective-permute-start = (f32[80,128]{1,0:T(8,128)S(1)}, f32[80,128]{1,0:T(8,128)S(1)}, u32[]{:S(2)}, u32[]{:S(2)}) collective-permute-start(f32[80,128]{1,0:T(8,128)S(1)} %get-tuple-element.34), channel_id=1, source_target_pairs={{0,2},{1,3},{2,4},{3,5},{4,6},{5,7},{6,14},{7,15},{14,12},{15,13},... | collective-permute-start | bytes 122888 | tf_op jit(solution)/shard_map/ppermute | solution.py:711
  39.3 3.3 %collective-permute-start.1 = (f32[80,128]{1,0:T(8,128)S(1)}, f32[80,128]{1,0:T(8,128)S(1)}, u32[]{:S(2)}, u32[]{:S(2)}) collective-permute-start(f32[80,128]{1,0:T(8,128)S(1)} %get-tuple-element.35), channel_id=1, source_target_pairs={{0,8},{1,9},{2,0},{3,1},{4,2},{5,3},{6,4},{7,5},{14,6},{15,7},{12,... | collective-permute-start | bytes 122888 | tf_op jit(solution)/shard_map/ppermute | solution.py:711
  44.8 6.9 %collective-permute-start.6 = (f32[2,5,2,8,128]{4,3,2,1,0:T(8,128)S(1)}, f32[2,5,2,8,128]{4,3,2,1,0:T(8,128)S(1)}, u32[]{:S(2)}, u32[]{:S(2)}) collective-permute-start(f32[2,5,2,8,128]{4,3,2,1,0:T(8,128)S(1)} %get-tuple-element.50), channel_id=1, source_target_pairs={{0,249},{1,24},{2,251},{3,26},{4,253},{5,28},{6,255},{7,30},{14,24... | collective-permute-start | bytes 245768 | tf_op jit(solution)/shard_map/ppermute | solution.py:711
  44.9 6.8 %collective-permute-start.7 = (f32[2,5,2,8,128]{4,3,2,1,0:T(8,128)S(1)}, f32[2,5,2,8,128]{4,3,2,1,0:T(8,128)S(1)}, u32[]{:S(2)}, u32[]{:S(2)}) collective-permute-start(f32[2,5,2,8,128]{4,3,2,1,0:T(8,128)S(1)} %get-tuple-element.51), channel_id=1, source_target_pairs={{0,1},{1,0},{2,3},{3,2},{4,5},{5,4},{6,7},{7,6},{14,15},{15,14},{1... | collective-permute-start | bytes 245768 | tf_op jit(solution)/shard_map/ppermute | solution.py:711
  48.6 3.1 %collective-permute-start.4 = (f32[80,128]{1,0:T(8,128)S(1)}, f32[80,128]{1,0:T(8,128)S(1)}, u32[]{:S(2)}, u32[]{:S(2)}) collective-permute-start(f32[80,128]{1,0:T(8,128)S(1)} %get-tuple-element.48), channel_id=1, source_target_pairs={{0,2},{1,3},{2,4},{3,5},{4,6},{5,7},{6,14},{7,15},{14,12},{15,13},... | collective-permute-start | bytes 122888 | tf_op jit(solution)/shard_map/ppermute | solution.py:711
  48.6 3.1 %collective-permute-start.5 = (f32[80,128]{1,0:T(8,128)S(1)}, f32[80,128]{1,0:T(8,128)S(1)}, u32[]{:S(2)}, u32[]{:S(2)}) collective-permute-start(f32[80,128]{1,0:T(8,128)S(1)} %get-tuple-element.49), channel_id=1, source_target_pairs={{0,8},{1,9},{2,0},{3,1},{4,2},{5,3},{6,4},{7,5},{14,6},{15,7},{12,... | collective-permute-start | bytes 122888 | tf_op jit(solution)/shard_map/ppermute | solution.py:711

commit v3 on v2

--- a/solution.py
+++ b/solution.py
@@ -145,6 +145,18 @@
         stores.append(pltpu.make_async_copy(source, target, stored.at[len(stores)]))
         stores[-1].start()
 
+    left = lax.broadcasted_iota(jnp.int32, (32, 128), 1) < 64
+    for p in range(3):
+        at = SHELL_ROWS + 8 * p
+        pieces = [received[device_of(m, part, row), at : at + 8, :] for part in range(2) for m in range(CHUNKS)]
+        around[...] = jnp.concatenate(pieces).T
+        for s in range(2 * p, min(2 * p + 2, SPECIES)):
+            low, high = [
+                around[pl.ds(pl.multiple_of(32 * lax.rem(column + 2 * (s - 2 * p) + h, 4), 32), 32), :] for h in range(2)
+            ]
+            coarse[s, 0:4] = jnp.where(left, low, pltpu.roll(high, 64, 1)).reshape(4, 8, 128)
+            coarse[s, 4:8] = jnp.where(left, pltpu.roll(low, 64, 1), high).reshape(4, 8, 128)
+    send(coarse, coarse_out)
     live = [table[OWN + 2 * k] > 0 for k in range(2)]
     high = [table[OWN + 2 * k + 1] > 0 for k in range(2)]
     in_plane = [jnp.where(high[k], lanes, 127 - lanes) < 2 for k in range(2)]
@@ -186,18 +198,6 @@
                 for j in range(2):
                     fine[k, s, x, 8 * j : 8 * j + 8, :] = jnp.where(live[k], tiles[j], 0.0)
             send(fine.at[k, s], fine_out.at[k, s])
-    left = lax.broadcasted_iota(jnp.int32, (32, 128), 1) < 64
-    for p in range(3):
-        at = SHELL_ROWS + 8 * p
-        pieces = [received[device_of(m, part, row), at : at + 8, :] for part in range(2) for m in range(CHUNKS)]
-        around[...] = jnp.concatenate(pieces).T
-        for s in range(2 * p, min(2 * p + 2, SPECIES)):
-            low, high = [
-                around[pl.ds(pl.multiple_of(32 * lax.rem(column + 2 * (s - 2 * p) + h, 4), 32), 32), :] for h in range(2)
-            ]
-            coarse[s, 0:4] = jnp.where(left, low, pltpu.roll(high, 64, 1)).reshape(4, 8, 128)
-            coarse[s, 4:8] = jnp.where(left, pltpu.roll(low, 64, 1), high).reshape(4, 8, 128)
-    send(coarse, coarse_out)
     for store in stores:
         store.wait()
 
@@ -600,7 +600,7 @@
                 out[t // 2, pl.ds(PLANE_ROWS + 8 * k + 2 * s, 2), :] = plane
         return carry
 
-    lax.fori_loop(0, BOXES, pack_box, 0, unroll=4)
+    lax.fori_loop(0, BOXES, pack_box, 0, unroll=8)
     mean_matrix = summing(lambda given_y, fine_y: fine_y // 2 == given_y)
 
     def open_z(high, row, source, old_source, rate_out, rate_in, sign):

time: 76 us -> 76.3 us (level)
  no operation moved by 1% of the time
where the time goes in v3:
time: 76.3 us; the launch traced here: 76.1 us
  blocking collectives  46 us (60%)
  starting transfers between devices  14.5 us (19%)
  Pallas kernels  14.1 us (18%)
  between operations  0.87 us (1%)
    all_to_all x2, blocking collectives, spread(): return lax.all_to_all(pieces, 'gy', 0, 0, tiled=True)  46 us
    ppermute x8, starting transfers between devices, exchange(): lax.ppermute(value, axes, [(device(*d), device(*target(*d))) for d in all...  14.5 us
    pallas_call x7, Pallas kernels, call(): pl.pallas_call(kernel, out_shape=out_shape, in_specs=[SMEM] * smem + [in_...  14.1 us
  transfers between devices with their start and end apart: 8, of which 1 were waited for; matrix products, arithmetic and copies ran while one was open for 0% of the time, Pallas kernels for 4%

profile of v3, /device:TPU:1, one launch (start us, length us, event | category | flops | bytes accessed | tf_op | source)
XLA Modules:
  0.0 76.1 jit_solution(2251789967122028082)
XLA Ops:
  0.6 2.7 %shard_map.77 = (f32[16,184,128]{2,1,0:T(8,128)S(1)}, s32[164]{0:T(256)S(1)}) custom-call(s32[3,512]{1,0:T(4,128)} %bitcast.3, s32[6,512]{1,0:T(8,128)} %bitcast.2, f32[5,8,8,128]{3,2,1,0:T(8,128)} %coarse_in.1, f32[2,5,16,16,128]{4,3,2,1,0:T(8,128)} %fine), custom_call_target="tpu_custom_call" | custom-call | tf_op jit(solution)/shard_map/pallas_call | solution.py:697
  3.3 27.0 %all_to_all.10.received = f32[16,184,128]{2,1,0:T(8,128)S(1)} all-to-all(f32[16,184,128]{2,1,0:T(8,128)S(1)} %get-tuple-element.29), channel_id=1, replica_groups=mesh['gx'=16,'gy'=16] {'gy'}, dimensions={0} | all-to-all | bytes 3014656 | tf_op jit(solution)/shard_map/all_to_all | solution.py:720
  30.3 0.0 copy-start
  30.3 0.0 copy-start.1
  30.3 0.0 copy-start.2
  30.3 0.9 %shard_map.78 = (f32[8,5,8,128]{3,2,1,0:T(8,128)S(1)}, f32[8,5,8,128]{3,2,1,0:T(8,128)S(1)}, f32[4,5,2,8,128]{4,3,2,1,0:T(8,128)S(1)}, f32[80,128]{1,0:T(8,128)S...) custom-call(s32[164]{0:T(256)S(1)} %get-tuple-element.28.table, ...), custom_call_target="tpu_custom_call" | custom-call | tf_op jit(solution)/shard_map/pallas_call | solution.py:697
  31.3 2.7 %collective-permute-start.2 = (f32[2,5,2,8,128]{4,3,2,1,0:T(8,128)S(1)}, f32[2,5,2,8,128]{4,3,2,1,0:T(8,128)S(1)}, u32[]{:S(2)}, u32[]{:S(2)}) collective-permute-start(f32[2,5,2,8,128]{4,3,2,1,0:T(8,128)S(1)} %get-tuple-element.36), channel_id=1, source_target_pairs={{0,249},{1,24},{2,251},{3,26},{4,253},{5,28},{6,255},{7,30},{14,24... | collective-permute-start | bytes 245768 | tf_op jit(solution)/shard_map/ppermute | solution.py:711
  33.9 5.2 %collective-permute-start.3 = (f32[2,5,2,8,128]{4,3,2,1,0:T(8,128)S(1)}, f32[2,5,2,8,128]{4,3,2,1,0:T(8,128)S(1)}, u32[]{:S(2)}, u32[]{:S(2)}) collective-permute-start(f32[2,5,2,8,128]{4,3,2,1,0:T(8,128)S(1)} %get-tuple-element.37), channel_id=1, source_target_pairs={{0,1},{1,0},{2,3},{3,2},{4,5},{5,4},{6,7},{7,6},{14,15},{15,14},{1... | collective-permute-start | bytes 245768 | tf_op jit(solution)/shard_map/ppermute | solution.py:711
  39.1 0.2 collective-permute-start
  39.3 1.3 %collective-permute-start.1 = (f32[80,128]{1,0:T(8,128)S(1)}, f32[80,128]{1,0:T(8,128)S(1)}, u32[]{:S(2)}, u32[]{:S(2)}) collective-permute-start(f32[80,128]{1,0:T(8,128)S(1)} %get-tuple-element.35), channel_id=1, source_target_pairs={{0,8},{1,9},{2,0},{3,1},{4,2},{5,3},{6,4},{7,5},{14,6},{15,7},{12,... | collective-permute-start | bytes 122888 | tf_op jit(solution)/shard_map/ppermute | solution.py:711
  40.6 0.0 copy-done
  40.6 0.0 copy-done.1
  40.6 0.0 copy-done.2
  40.6 2.0 %shard_map.79.interior = f32[2,5,16,16,128]{4,3,2,1,0:T(8,128)S(1)} custom-call(f32[3,5]{1,0:T(4,128)S(1)} %copy-done.2, f32[5,5]{1,0:T(8,128)S(1)} %copy-done.1, f32[2,5,16,16,128]{4,3,2,1,0:T(8,128)S(1)} %copy-done), custom_call_target="tpu_custom_call" | custom-call | tf_op jit(solution)/shard_map/pallas_call | solution.py:697
  42.6 0.0 collective-permute-done.below.old_below
  42.6 0.0 collective-permute-done.1.above.old_above
  42.6 0.0 collective-permute-done.2.outer.old_outer
  42.6 0.0 collective-permute-done.3.inner.old_inner
  42.6 2.2 %shard_map.80 = (f32[8,5,8,128]{3,2,1,0:T(8,128)S(1)}, f32[8,5,8,128]{3,2,1,0:T(8,128)S(1)}, f32[4,5,2,8,128]{4,3,2,1,0:T(8,128)S(1)}, f32[4,5,2,8,128]{4,3,2,1,...) custom-call(s32[164]{0:T(256)S(1)} %get-tuple-element.28.table, ...), custom_call_target="tpu_custom_call" | custom-call | tf_op jit(solution)/shard_map/pallas_call | solution.py:697
  44.8 0.1 collective-permute-start.6
  44.9 3.7 %collective-permute-start.7 = (f32[2,5,2,8,128]{4,3,2,1,0:T(8,128)S(1)}, f32[2,5,2,8,128]{4,3,2,1,0:T(8,128)S(1)}, u32[]{:S(2)}, u32[]{:S(2)}) collective-permute-start(f32[2,5,2,8,128]{4,3,2,1,0:T(8,128)S(1)} %get-tuple-element.51), channel_id=1, source_target_pairs={{0,1},{1,0},{2,3},{3,2},{4,5},{5,4},{6,7},{7,6},{14,15},{15,14},{1... | collective-permute-start | bytes 245768 | tf_op jit(solution)/shard_map/ppermute | solution.py:711
  48.6 0.0 collective-permute-start.4
  48.6 1.4 %collective-permute-start.5 = (f32[80,128]{1,0:T(8,128)S(1)}, f32[80,128]{1,0:T(8,128)S(1)}, u32[]{:S(2)}, u32[]{:S(2)}) collective-permute-start(f32[80,128]{1,0:T(8,128)S(1)} %get-tuple-element.49), channel_id=1, source_target_pairs={{0,8},{1,9},{2,0},{3,1},{4,2},{5,3},{6,4},{7,5},{14,6},{15,7},{12,... | collective-permute-start | bytes 122888 | tf_op jit(solution)/shard_map/ppermute | solution.py:711
  50.1 1.1 %shard_map.81.corrected = f32[4,5,2,8,128]{4,3,2,1,0:T(8,128)S(1)} custom-call(s32[164]{0:T(256)S(1)} %get-tuple-element.28.table, f32[3,5]{1,0:T(4,128)S(1)} %copy-done.2, f32[8,5,8,128]{3,2,1,0:T(8,128)S(1)} %get-tuple-element.38.fine0.old0, f32[8,5,8,128]{3,2,1,0:T(8,128)S(1)} %get-tuple-element.39.fine1.old1, ...), custom_call_target="tpu_custom_call" | custom-call | tf_op jit(solution)/shard_map/pallas_call | solution.py:697
  51.2 0.5 collective-permute-done.4.below
  51.7 0.0 collective-permute-done.5.above
  51.8 0.0 collective-permute-done.6.outer
  51.8 0.0 collective-permute-done.7.inner
  51.8 2.9 %shard_map.82 = f32[16,120,128]{2,1,0:T(8,128)S(1)} custom-call(s32[164]{0:T(256)S(1)} %get-tuple-element.28.table, f32[3,5]{1,0:T(4,128)S(1)} %copy-done.2, f32[5,5]{1,0:T(8,128)S(1)} %copy-done.1, f32[8,5,8,128]{3,2,1,0:T(8,128)S(1)} %get-tuple-element.38.fine0.old0, f32[8,5,8,128]{3,2,1,0:T(8,128)S(1)} %get-tuple-element.39.fine1.old1, ...), custom_call_target="tpu_custom_call" | custom-call | tf_op jit(solution)/shard_map/pallas_call | solution.py:697
  54.6 19.0 %all_to_all.11.received = f32[16,120,128]{2,1,0:T(8,128)S(1)} all-to-all(f32[16,120,128]{2,1,0:T(8,128)S(1)} %shard_map.82), channel_id=1, replica_groups=mesh['gx'=16,'gy'=16] {'gy'}, dimensions={0} | all-to-all | bytes 1966080 | tf_op jit(solution)/shard_map/all_to_all | solution.py:720
  73.6 2.3 %shard_map.83 = (f32[5,8,8,128]{3,2,1,0:T(8,128)}, f32[2,5,16,16,128]{4,3,2,1,0:T(8,128)}) custom-call(s32[164]{0:T(256)S(1)} %get-tuple-element.28.table, f32[16,120,128]{2,1,0:T(8,128)S(1)} %all_to_all.11.received, f32[2,5,16,16,128]{4,3,2,1,0:T(8,128)S(1)} %shard_map.79.interior), custom_call_target="tpu_custom_call" | custom-call | tf_op jit(solution)/shard_map/pallas_call | solution.py:697
Async XLA Ops:
  30.3 10.2 %copy-start = (f32[2,5,16,16,128]{4,3,2,1,0:T(8,128)S(1)}, f32[2,5,16,16,128]{4,3,2,1,0:T(8,128)}, u32[]{:S(2)}) copy-start(f32[2,5,16,16,128]{4,3,2,1,0:T(8,128)} %fine) | copy-start | bytes 3932164
  30.3 10.2 %copy-start.1 = (f32[5,5]{1,0:T(8,128)S(1)}, f32[5,5]{1,0:T(8,128)}, u32[]{:S(2)}) copy-start(f32[5,5]{1,0:T(8,128)} %reaction.5) | copy-start | bytes 304
  30.3 10.2 %copy-start.2 = (f32[3,5]{1,0:T(4,128)S(1)}, f32[3,5]{1,0:T(4,128)}, u32[]{:S(2)}) copy-start(f32[3,5]{1,0:T(4,128)} %courant.7) | copy-start | bytes 184
  31.3 11.3 %collective-permute-start.2 = (f32[2,5,2,8,128]{4,3,2,1,0:T(8,128)S(1)}, f32[2,5,2,8,128]{4,3,2,1,0:T(8,128)S(1)}, u32[]{:S(2)}, u32[]{:S(2)}) collective-permute-start(f32[2,5,2,8,128]{4,3,2,1,0:T(8,128)S(1)} %get-tuple-element.36), channel_id=1, source_target_pairs={{0,249},{1,24},{2,251},{3,26},{4,253},{5,28},{6,255},{7,30},{14,24... | collective-permute-start | bytes 245768 | tf_op jit(solution)/shard_map/ppermute | solution.py:711
  33.9 8.7 %collective-permute-start.3 = (f32[2,5,2,8,128]{4,3,2,1,0:T(8,128)S(1)}, f32[2,5,2,8,128]{4,3,2,1,0:T(8,128)S(1)}, u32[]{:S(2)}, u32[]{:S(2)}) collective-permute-start(f32[2,5,2,8,128]{4,3,2,1,0:T(8,128)S(1)} %get-tuple-element.37), channel_id=1, source_target_pairs={{0,1},{1,0},{2,3},{3,2},{4,5},{5,4},{6,7},{7,6},{14,15},{15,14},{1... | collective-permute-start | bytes 245768 | tf_op jit(solution)/shard_map/ppermute | solution.py:711
  39.1 3.5 %collective-permute-start = (f32[80,128]{1,0:T(8,128)S(1)}, f32[80,128]{1,0:T(8,128)S(1)}, u32[]{:S(2)}, u32[]{:S(2)}) collective-permute-start(f32[80,128]{1,0:T(8,128)S(1)} %get-tuple-element.34), channel_id=1, source_target_pairs={{0,2},{1,3},{2,4},{3,5},{4,6},{5,7},{6,14},{7,15},{14,12},{15,13},... | collective-permute-start | bytes 122888 | tf_op jit(solution)/shard_map/ppermute | solution.py:711
  39.3 3.3 %collective-permute-start.1 = (f32[80,128]{1,0:T(8,128)S(1)}, f32[80,128]{1,0:T(8,128)S(1)}, u32[]{:S(2)}, u32[]{:S(2)}) collective-permute-start(f32[80,128]{1,0:T(8,128)S(1)} %get-tuple-element.35), channel_id=1, source_target_pairs={{0,8},{1,9},{2,0},{3,1},{4,2},{5,3},{6,4},{7,5},{14,6},{15,7},{12,... | collective-permute-start | bytes 122888 | tf_op jit(solution)/shard_map/ppermute | solution.py:711
  44.8 6.9 %collective-permute-start.6 = (f32[2,5,2,8,128]{4,3,2,1,0:T(8,128)S(1)}, f32[2,5,2,8,128]{4,3,2,1,0:T(8,128)S(1)}, u32[]{:S(2)}, u32[]{:S(2)}) collective-permute-start(f32[2,5,2,8,128]{4,3,2,1,0:T(8,128)S(1)} %get-tuple-element.50), channel_id=1, source_target_pairs={{0,249},{1,24},{2,251},{3,26},{4,253},{5,28},{6,255},{7,30},{14,24... | collective-permute-start | bytes 245768 | tf_op jit(solution)/shard_map/ppermute | solution.py:711
  44.9 6.8 %collective-permute-start.7 = (f32[2,5,2,8,128]{4,3,2,1,0:T(8,128)S(1)}, f32[2,5,2,8,128]{4,3,2,1,0:T(8,128)S(1)}, u32[]{:S(2)}, u32[]{:S(2)}) collective-permute-start(f32[2,5,2,8,128]{4,3,2,1,0:T(8,128)S(1)} %get-tuple-element.51), channel_id=1, source_target_pairs={{0,1},{1,0},{2,3},{3,2},{4,5},{5,4},{6,7},{7,6},{14,15},{15,14},{1... | collective-permute-start | bytes 245768 | tf_op jit(solution)/shard_map/ppermute | solution.py:711
  48.6 3.1 %collective-permute-start.4 = (f32[80,128]{1,0:T(8,128)S(1)}, f32[80,128]{1,0:T(8,128)S(1)}, u32[]{:S(2)}, u32[]{:S(2)}) collective-permute-start(f32[80,128]{1,0:T(8,128)S(1)} %get-tuple-element.48), channel_id=1, source_target_pairs={{0,2},{1,3},{2,4},{3,5},{4,6},{5,7},{6,14},{7,15},{14,12},{15,13},... | collective-permute-start | bytes 122888 | tf_op jit(solution)/shard_map/ppermute | solution.py:711
  48.6 3.1 %collective-permute-start.5 = (f32[80,128]{1,0:T(8,128)S(1)}, f32[80,128]{1,0:T(8,128)S(1)}, u32[]{:S(2)}, u32[]{:S(2)}) collective-permute-start(f32[80,128]{1,0:T(8,128)S(1)} %get-tuple-element.49), channel_id=1, source_target_pairs={{0,8},{1,9},{2,0},{3,1},{4,2},{5,3},{6,4},{7,5},{14,6},{15,7},{12,... | collective-permute-start | bytes 122888 | tf_op jit(solution)/shard_map/ppermute | solution.py:711
